TPU v7x, 256 devices: a whole 4x4x8 slice. The times are simulated.
256 devices in a mesh: band: 8 (over z_hi, core), plane: 32 (over x, y, z_lo).
Axes of the slice: x: 4, y: 4, z: 8 (z_hi: 4, z_lo: 2; z = z_hi * 2 + z_lo), core: 2. Of those that a mesh axis runs over, the one named last changes fastest.
Arguments:
- targets: float32 [16, 128, 128, 128], P('band', 'plane'), may hold values from -6 to 6
- sources: float32 [8, 128, 128, 128], P('band', 'plane'), may hold values from -6 to 6
- kernel: float32 [128, 128, 128], P(None, 'plane'), as said below
Outputs:
- fock_applied: float32 [16, 128, 128, 128], P('band', 'plane')
Inputs may be any that keep to these rules, and one draw needn't show every extreme that they name: kernel is positive and even: kernel[a, b, c] equals kernel[(-a) mod 128, (-b) mod 128, (-c) mod 128].
All inputs are finite; a program needn't handle non-finite values.
Results may differ from a plain program's by a relative error of at most 0.0001.
Values sent between devices are 32-bit elements; how exact they have to be, the bound alone decides.
No kernel may reach another device: no remote copies, remote signals or barrier semaphores. Data moves between devices by JAX's collectives and lax.ppermute only.
A program may use at most 64 MiB of HBM per device.

v0:
```python
import math

import jax
import jax.numpy as jnp
from jax import lax
from jax.sharding import PartitionSpec as P

exact_share = 0.25
finest = lax.Precision.HIGHEST
z_pattern = "pabn,nk->pabk"
y_pattern = "panc,nk->pakc"
x_pattern = "pnbc,nk->pkbc"


def dft_tables(length):
    indices = jnp.arange(length, dtype=jnp.int32)
    product_mod = indices[:, None] * indices[None, :] % length
    angles = product_mod.astype(jnp.float32) * (2.0 * math.pi / length)
    return (jnp.cos(angles), jnp.sin(angles))


def transform_axis(values, pattern, matrix):
    return jnp.einsum(pattern, values, matrix, precision=finest)


def forward(real_part, imag_part, pattern, cosine_table, sine_table):
    if imag_part is None:
        return (
            transform_axis(real_part, pattern, cosine_table),
            -transform_axis(real_part, pattern, sine_table),
        )
    new_real = transform_axis(real_part, pattern, cosine_table) + transform_axis(
        imag_part, pattern, sine_table
    )
    new_imag = transform_axis(imag_part, pattern, cosine_table) - transform_axis(
        real_part, pattern, sine_table
    )
    return (new_real, new_imag)


def inverse(real_part, imag_part, pattern, cosine_table, sine_table):
    new_real = transform_axis(real_part, pattern, cosine_table) - transform_axis(
        imag_part, pattern, sine_table
    )
    new_imag = transform_axis(imag_part, pattern, cosine_table) + transform_axis(
        real_part, pattern, sine_table
    )
    return (new_real, new_imag)


def potentials(real_part, imag_part, kernel_scaled, cosine_table, sine_table):
    real_part, imag_part = forward(real_part, imag_part, z_pattern, cosine_table, sine_table)
    real_part, imag_part = forward(real_part, imag_part, y_pattern, cosine_table, sine_table)
    first, second = forward(
        lax.all_to_all(real_part, "plane", split_axis=2, concat_axis=1, tiled=True),
        lax.all_to_all(imag_part, "plane", split_axis=2, concat_axis=1, tiled=True),
        x_pattern,
        cosine_table,
        sine_table,
    )
    first = first * kernel_scaled[None]
    second = second * kernel_scaled[None]
    first, second = inverse(first, second, x_pattern, cosine_table, sine_table)
    real_part = lax.all_to_all(first, "plane", split_axis=1, concat_axis=2, tiled=True)
    imag_part = lax.all_to_all(second, "plane", split_axis=1, concat_axis=2, tiled=True)
    return inverse(real_part, imag_part, y_pattern, cosine_table, sine_table)


def pair_potentials(density, kernel_scaled, cosine_table, sine_table):
    real_part, imag_part = potentials(density, None, kernel_scaled, cosine_table, sine_table)
    return transform_axis(real_part, z_pattern, cosine_table) - transform_axis(
        imag_part, z_pattern, sine_table
    )


def on_device(targets, sources, kernel):
    everyone = lax.all_gather(sources, "band", axis=0, tiled=True)
    length = targets.shape[-1]
    cosine_table, sine_table = dft_tables(length)
    kernel_scaled = kernel * (1.0 / float(length) ** 3)
    source_count = everyone.shape[0]

    def accumulate(position, summed):
        source = lax.dynamic_index_in_dim(everyone, position, 0, keepdims=False)
        potential = pair_potentials(targets * source[None], kernel_scaled, cosine_table, sine_table)
        return summed + potential * source[None]

    summed = lax.fori_loop(0, source_count, accumulate, jnp.zeros_like(targets))
    return -exact_share * summed


def solution(mesh):
    return jax.shard_map(
        on_device,
        mesh=mesh,
        in_specs=(
            P("band", "plane", None, None),
            P("band", "plane", None, None),
            P(None, "plane", None),
        ),
        out_specs=P("band", "plane", None, None),
        check_vma=False,
    )
```

profile of v0, /device:TPU:8, one launch (start us, length us, event | category | flops | bytes accessed | tf_op | source)
XLA Modules:
  0.0 715.8 jit_solution(5670941927282722492)
XLA Ops:
  8.4 40.3 %all-gather.2.cloned.1.call-done = f32[8,4,128,128]{3,2,1,0:T(8,128)} async-done(((f32[1,4,128,128]{3,2,1,0:T(8,128)}), f32[8,4,128,128]{3,2,1,0:T(8,128)}) %all-gather.2.cloned.1.call-update) | async-done | bytes 2097168 | tf_op jit(solution)/shard_map/all_gather | solution.py:77
  48.7 659.4 %while.15 = (s32[]{:T(128)}, f32[2,4,128,128]{3,2,1,0:T(8,128)S(1)}, f32[8,4,128,128]{3,2,1,0:T(8,128)}, f32[2,4,128,128]{3,2,1,0:T(8,128)}, f32[128,4,128]{0,2,1:T(8,128)S(1)}, /*index=5*/s32[]{:T(128)}, s32[]{:T(128)}) while((s32[]{:T(128)}, f32[2,4,128,128]{3,2,1,0:T(8,128)S(1)}, f32[8,4,128,128]{3,2,1,0:T(8,128)}, ...), condition=%wide.region_1.2_spmd.clone.clone, body=%wide.region_0.1_spmd.clone.clone.sunk | while | flops 4033347584 | bytes 49021180 | solution.py:88
  55.4 7.4 %all-to-all-start = ((f32[2,4,128,128]{3,1,0,2:T(4,128)}), f32[2,4,128,128]{3,1,0,2:T(4,128)S(1)}, u32[]{:S(2)}, u32[]{:S(2)}) async-start(f32[2,4,128,128]{3,1,0,2:T(4,128)} %copy.82), calls=%async_computation | async-start | bytes 1048576 | tf_op jit(solution)/shard_map/while/body/eval_jaxpr/all_to_all | solution.py:55
  65.8 8.5 %all-to-all-done = f32[2,4,128,128]{3,1,0,2:T(4,128)S(1)} async-done(((f32[2,4,128,128]{3,1,0,2:T(4,128)}), f32[2,4,128,128]{3,1,0,2:T(4,128)S(1)}, u32[]{:S(2)}, u32[]{:S(2)}) %all-to-all-start) | async-done | bytes 524320 | tf_op jit(solution)/shard_map/while/body/eval_jaxpr/all_to_all | solution.py:55
  74.3 5.0 all-to-all-start.1
  79.7 9.9 %all-to-all-done.1 = f32[2,4,128,128]{3,1,0,2:T(4,128)S(1)} async-done(((f32[2,4,128,128]{3,1,0,2:T(4,128)}), f32[2,4,128,128]{3,1,0,2:T(4,128)S(1)}, u32[]{:S(2)}, u32[]{:S(2)}) %all-to-all-start.1) | async-done | bytes 524320 | tf_op jit(solution)/shard_map/while/body/eval_jaxpr/all_to_all | solution.py:56
  97.3 5.0 all-to-all-start.2
  105.0 7.1 all-to-all-done.2
  112.1 5.0 all-to-all-start.3
  117.5 9.3 %all-to-all-done.3 = f32[2,128,4,128]{3,2,0,1:T(4,128)S(1)} async-done(((f32[2,128,4,128]{3,2,0,1:T(4,128)}), f32[2,128,4,128]{3,2,0,1:T(4,128)S(1)}, u32[]{:S(2)}, u32[]{:S(2)}) %all-to-all-start.3) | async-done | bytes 524320 | tf_op jit(solution)/shard_map/while/body/eval_jaxpr/all_to_all | solution.py:65
  141.1 5.0 all-to-all-start
  149.0 6.8 all-to-all-done
  155.8 5.0 all-to-all-start.1
  161.3 9.3 %all-to-all-done.1 = f32[2,4,128,128]{3,1,0,2:T(4,128)S(1)} async-done(((f32[2,4,128,128]{3,1,0,2:T(4,128)}), f32[2,4,128,128]{3,1,0,2:T(4,128)S(1)}, u32[]{:S(2)}, u32[]{:S(2)}) %all-to-all-start.1) | async-done | bytes 524320 | tf_op jit(solution)/shard_map/while/body/eval_jaxpr/all_to_all | solution.py:56
  178.3 5.0 all-to-all-start.2
  186.0 7.1 all-to-all-done.2
  193.1 5.0 all-to-all-start.3
  198.6 9.3 %all-to-all-done.3 = f32[2,128,4,128]{3,2,0,1:T(4,128)S(1)} async-done(((f32[2,128,4,128]{3,2,0,1:T(4,128)}), f32[2,128,4,128]{3,2,0,1:T(4,128)S(1)}, u32[]{:S(2)}, u32[]{:S(2)}) %all-to-all-start.3) | async-done | bytes 524320 | tf_op jit(solution)/shard_map/while/body/eval_jaxpr/all_to_all | solution.py:65
  222.1 5.0 all-to-all-start
  230.0 7.1 all-to-all-done
  242.5 9.3 %all-to-all-done.1 = f32[2,4,128,128]{3,1,0,2:T(4,128)S(1)} async-done(((f32[2,4,128,128]{3,1,0,2:T(4,128)}), f32[2,4,128,128]{3,1,0,2:T(4,128)S(1)}, u32[]{:S(2)}, u32[]{:S(2)}) %all-to-all-start.1) | async-done | bytes 524320 | tf_op jit(solution)/shard_map/while/body/eval_jaxpr/all_to_all | solution.py:56
  259.5 5.0 all-to-all-start.2
  267.1 7.9 %all-to-all-done.2 = f32[2,128,4,128]{3,2,0,1:T(4,128)S(1)} async-done(((f32[2,128,4,128]{3,2,0,1:T(4,128)}), f32[2,128,4,128]{3,2,0,1:T(4,128)S(1)}, u32[]{:S(2)}, u32[]{:S(2)}) %all-to-all-start.2) | async-done | bytes 524320 | tf_op jit(solution)/shard_map/while/body/eval_jaxpr/all_to_all | solution.py:64
  275.0 5.0 all-to-all-start.3
  280.5 9.3 %all-to-all-done.3 = f32[2,128,4,128]{3,2,0,1:T(4,128)S(1)} async-done(((f32[2,128,4,128]{3,2,0,1:T(4,128)}), f32[2,128,4,128]{3,2,0,1:T(4,128)S(1)}, u32[]{:S(2)}, u32[]{:S(2)}) %all-to-all-start.3) | async-done | bytes 524320 | tf_op jit(solution)/shard_map/while/body/eval_jaxpr/all_to_all | solution.py:65
  304.0 5.0 all-to-all-start
  312.0 9.3 %all-to-all-done = f32[2,4,128,128]{3,1,0,2:T(4,128)S(1)} async-done(((f32[2,4,128,128]{3,1,0,2:T(4,128)}), f32[2,4,128,128]{3,1,0,2:T(4,128)S(1)}, u32[]{:S(2)}, u32[]{:S(2)}) %all-to-all-start) | async-done | bytes 524320 | tf_op jit(solution)/shard_map/while/body/eval_jaxpr/all_to_all | solution.py:55
  321.3 5.0 all-to-all-start.1
  326.7 9.3 %all-to-all-done.1 = f32[2,4,128,128]{3,1,0,2:T(4,128)S(1)} async-done(((f32[2,4,128,128]{3,1,0,2:T(4,128)}), f32[2,4,128,128]{3,1,0,2:T(4,128)S(1)}, u32[]{:S(2)}, u32[]{:S(2)}) %all-to-all-start.1) | async-done | bytes 524320 | tf_op jit(solution)/shard_map/while/body/eval_jaxpr/all_to_all | solution.py:56
  343.7 5.0 all-to-all-start.2
  351.4 7.4 %all-to-all-done.2 = f32[2,128,4,128]{3,2,0,1:T(4,128)S(1)} async-done(((f32[2,128,4,128]{3,2,0,1:T(4,128)}), f32[2,128,4,128]{3,2,0,1:T(4,128)S(1)}, u32[]{:S(2)}, u32[]{:S(2)}) %all-to-all-start.2) | async-done | bytes 524320 | tf_op jit(solution)/shard_map/while/body/eval_jaxpr/all_to_all | solution.py:64
  358.8 5.0 all-to-all-start.3
  364.2 9.3 %all-to-all-done.3 = f32[2,128,4,128]{3,2,0,1:T(4,128)S(1)} async-done(((f32[2,128,4,128]{3,2,0,1:T(4,128)}), f32[2,128,4,128]{3,2,0,1:T(4,128)S(1)}, u32[]{:S(2)}, u32[]{:S(2)}) %all-to-all-start.3) | async-done | bytes 524320 | tf_op jit(solution)/shard_map/while/body/eval_jaxpr/all_to_all | solution.py:65
  387.8 5.0 all-to-all-start
  395.7 6.8 all-to-all-done
  402.5 5.0 all-to-all-start.1
  408.0 10.2 %all-to-all-done.1 = f32[2,4,128,128]{3,1,0,2:T(4,128)S(1)} async-done(((f32[2,4,128,128]{3,1,0,2:T(4,128)}), f32[2,4,128,128]{3,1,0,2:T(4,128)S(1)}, u32[]{:S(2)}, u32[]{:S(2)}) %all-to-all-start.1) | async-done | bytes 524320 | tf_op jit(solution)/shard_map/while/body/eval_jaxpr/all_to_all | solution.py:56
  425.8 5.0 all-to-all-start.2
  433.5 7.1 all-to-all-done.2
  440.6 5.0 all-to-all-start.3
  446.1 9.3 %all-to-all-done.3 = f32[2,128,4,128]{3,2,0,1:T(4,128)S(1)} async-done(((f32[2,128,4,128]{3,2,0,1:T(4,128)}), f32[2,128,4,128]{3,2,0,1:T(4,128)S(1)}, u32[]{:S(2)}, u32[]{:S(2)}) %all-to-all-start.3) | async-done | bytes 524320 | tf_op jit(solution)/shard_map/while/body/eval_jaxpr/all_to_all | solution.py:65
  469.6 5.0 all-to-all-start
  477.6 6.8 all-to-all-done
  484.4 5.0 all-to-all-start.1
  489.9 9.5 %all-to-all-done.1 = f32[2,4,128,128]{3,1,0,2:T(4,128)S(1)} async-done(((f32[2,4,128,128]{3,1,0,2:T(4,128)}), f32[2,4,128,128]{3,1,0,2:T(4,128)S(1)}, u32[]{:S(2)}, u32[]{:S(2)}) %all-to-all-start.1) | async-done | bytes 524320 | tf_op jit(solution)/shard_map/while/body/eval_jaxpr/all_to_all | solution.py:56
  507.0 5.0 all-to-all-start.2
  514.7 7.1 all-to-all-done.2
  521.8 5.0 all-to-all-start.3
  527.3 10.5 %all-to-all-done.3 = f32[2,128,4,128]{3,2,0,1:T(4,128)S(1)} async-done(((f32[2,128,4,128]{3,2,0,1:T(4,128)}), f32[2,128,4,128]{3,2,0,1:T(4,128)S(1)}, u32[]{:S(2)}, u32[]{:S(2)}) %all-to-all-start.3) | async-done | bytes 524320 | tf_op jit(solution)/shard_map/while/body/eval_jaxpr/all_to_all | solution.py:65
  552.0 4.9 all-to-all-start
  559.9 6.8 all-to-all-done
  566.7 5.0 all-to-all-start.1
  572.2 9.4 %all-to-all-done.1 = f32[2,4,128,128]{3,1,0,2:T(4,128)S(1)} async-done(((f32[2,4,128,128]{3,1,0,2:T(4,128)}), f32[2,4,128,128]{3,1,0,2:T(4,128)S(1)}, u32[]{:S(2)}, u32[]{:S(2)}) %all-to-all-start.1) | async-done | bytes 524320 | tf_op jit(solution)/shard_map/while/body/eval_jaxpr/all_to_all | solution.py:56
  596.8 7.1 all-to-all-done.2
  603.9 5.0 all-to-all-start.3
  609.4 9.3 %all-to-all-done.3 = f32[2,128,4,128]{3,2,0,1:T(4,128)S(1)} async-done(((f32[2,128,4,128]{3,2,0,1:T(4,128)}), f32[2,128,4,128]{3,2,0,1:T(4,128)S(1)}, u32[]{:S(2)}, u32[]{:S(2)}) %all-to-all-start.3) | async-done | bytes 524320 | tf_op jit(solution)/shard_map/while/body/eval_jaxpr/all_to_all | solution.py:65
  632.9 5.0 all-to-all-start
  640.9 7.0 all-to-all-done
  647.9 5.0 all-to-all-start.1
  653.4 10.1 %all-to-all-done.1 = f32[2,4,128,128]{3,1,0,2:T(4,128)S(1)} async-done(((f32[2,4,128,128]{3,1,0,2:T(4,128)}), f32[2,4,128,128]{3,1,0,2:T(4,128)S(1)}, u32[]{:S(2)}, u32[]{:S(2)}) %all-to-all-start.1) | async-done | bytes 524320 | tf_op jit(solution)/shard_map/while/body/eval_jaxpr/all_to_all | solution.py:56
  671.1 5.0 all-to-all-start.2
  678.8 7.0 all-to-all-done.2
  685.9 5.0 all-to-all-start.3
  691.3 9.3 %all-to-all-done.3 = f32[2,128,4,128]{3,2,0,1:T(4,128)S(1)} async-done(((f32[2,128,4,128]{3,2,0,1:T(4,128)}), f32[2,128,4,128]{3,2,0,1:T(4,128)S(1)}, u32[]{:S(2)}, u32[]{:S(2)}) %all-to-all-start.3) | async-done | bytes 524320 | tf_op jit(solution)/shard_map/while/body/eval_jaxpr/all_to_all | solution.py:65
  (288 shorter events, 237.7 us)
Async XLA Ops:
  6.5 42.1 %all-gather.2.cloned.1.call-start = ((), (), s32[]{:S(2)}) async-start(), calls=%async_computation.4 | async-start | bytes 2359296 | tf_op jit(solution)/shard_map/all_gather | solution.py:77
  48.7 2.9 copy-start
  55.4 18.9 %all-to-all-start = ((f32[2,4,128,128]{3,1,0,2:T(4,128)}), f32[2,4,128,128]{3,1,0,2:T(4,128)S(1)}, u32[]{:S(2)}, u32[]{:S(2)}) async-start(f32[2,4,128,128]{3,1,0,2:T(4,128)} %copy.82), calls=%async_computation | async-start | bytes 1048576 | tf_op jit(solution)/shard_map/while/body/eval_jaxpr/all_to_all | solution.py:55
  74.3 15.4 %all-to-all-start.1 = ((f32[2,4,128,128]{3,1,0,2:T(4,128)}), f32[2,4,128,128]{3,1,0,2:T(4,128)S(1)}, u32[]{:S(2)}, u32[]{:S(2)}) async-start(f32[2,4,128,128]{3,1,0,2:T(4,128)} %copy.85), calls=%async_computation.1 | async-start | bytes 1048576 | tf_op jit(solution)/shard_map/while/body/eval_jaxpr/all_to_all | solution.py:56
  97.3 14.8 %all-to-all-start.2 = ((f32[2,128,4,128]{3,2,0,1:T(4,128)}), f32[2,128,4,128]{3,2,0,1:T(4,128)S(1)}, u32[]{:S(2)}, u32[]{:S(2)}) async-start(f32[2,128,4,128]{3,2,0,1:T(4,128)} %copy.88), calls=%async_computation.2 | async-start | bytes 1048576 | tf_op jit(solution)/shard_map/while/body/eval_jaxpr/all_to_all | solution.py:64
  112.1 14.8 %all-to-all-start.3 = ((f32[2,128,4,128]{3,2,0,1:T(4,128)}), f32[2,128,4,128]{3,2,0,1:T(4,128)S(1)}, u32[]{:S(2)}, u32[]{:S(2)}) async-start(f32[2,128,4,128]{3,2,0,1:T(4,128)} %copy.91), calls=%async_computation.3 | async-start | bytes 1048576 | tf_op jit(solution)/shard_map/while/body/eval_jaxpr/all_to_all | solution.py:65
  134.3 2.9 copy-start
  141.1 14.8 %all-to-all-start = ((f32[2,4,128,128]{3,1,0,2:T(4,128)}), f32[2,4,128,128]{3,1,0,2:T(4,128)S(1)}, u32[]{:S(2)}, u32[]{:S(2)}) async-start(f32[2,4,128,128]{3,1,0,2:T(4,128)} %copy.82), calls=%async_computation | async-start | bytes 1048576 | tf_op jit(solution)/shard_map/while/body/eval_jaxpr/all_to_all | solution.py:55
  155.8 14.8 %all-to-all-start.1 = ((f32[2,4,128,128]{3,1,0,2:T(4,128)}), f32[2,4,128,128]{3,1,0,2:T(4,128)S(1)}, u32[]{:S(2)}, u32[]{:S(2)}) async-start(f32[2,4,128,128]{3,1,0,2:T(4,128)} %copy.85), calls=%async_computation.1 | async-start | bytes 1048576 | tf_op jit(solution)/shard_map/while/body/eval_jaxpr/all_to_all | solution.py:56
  178.3 14.8 %all-to-all-start.2 = ((f32[2,128,4,128]{3,2,0,1:T(4,128)}), f32[2,128,4,128]{3,2,0,1:T(4,128)S(1)}, u32[]{:S(2)}, u32[]{:S(2)}) async-start(f32[2,128,4,128]{3,2,0,1:T(4,128)} %copy.88), calls=%async_computation.2 | async-start | bytes 1048576 | tf_op jit(solution)/shard_map/while/body/eval_jaxpr/all_to_all | solution.py:64
  193.1 14.8 %all-to-all-start.3 = ((f32[2,128,4,128]{3,2,0,1:T(4,128)}), f32[2,128,4,128]{3,2,0,1:T(4,128)S(1)}, u32[]{:S(2)}, u32[]{:S(2)}) async-start(f32[2,128,4,128]{3,2,0,1:T(4,128)} %copy.91), calls=%async_computation.3 | async-start | bytes 1048576 | tf_op jit(solution)/shard_map/while/body/eval_jaxpr/all_to_all | solution.py:65
  215.3 2.9 copy-start
  222.1 15.1 %all-to-all-start = ((f32[2,4,128,128]{3,1,0,2:T(4,128)}), f32[2,4,128,128]{3,1,0,2:T(4,128)S(1)}, u32[]{:S(2)}, u32[]{:S(2)}) async-start(f32[2,4,128,128]{3,1,0,2:T(4,128)} %copy.82), calls=%async_computation | async-start | bytes 1048576 | tf_op jit(solution)/shard_map/while/body/eval_jaxpr/all_to_all | solution.py:55
  237.1 14.7 %all-to-all-start.1 = ((f32[2,4,128,128]{3,1,0,2:T(4,128)}), f32[2,4,128,128]{3,1,0,2:T(4,128)S(1)}, u32[]{:S(2)}, u32[]{:S(2)}) async-start(f32[2,4,128,128]{3,1,0,2:T(4,128)} %copy.85), calls=%async_computation.1 | async-start | bytes 1048576 | tf_op jit(solution)/shard_map/while/body/eval_jaxpr/all_to_all | solution.py:56
  259.5 15.6 %all-to-all-start.2 = ((f32[2,128,4,128]{3,2,0,1:T(4,128)}), f32[2,128,4,128]{3,2,0,1:T(4,128)S(1)}, u32[]{:S(2)}, u32[]{:S(2)}) async-start(f32[2,128,4,128]{3,2,0,1:T(4,128)} %copy.88), calls=%async_computation.2 | async-start | bytes 1048576 | tf_op jit(solution)/shard_map/while/body/eval_jaxpr/all_to_all | solution.py:64
  275.0 14.7 %all-to-all-start.3 = ((f32[2,128,4,128]{3,2,0,1:T(4,128)}), f32[2,128,4,128]{3,2,0,1:T(4,128)S(1)}, u32[]{:S(2)}, u32[]{:S(2)}) async-start(f32[2,128,4,128]{3,2,0,1:T(4,128)} %copy.91), calls=%async_computation.3 | async-start | bytes 1048576 | tf_op jit(solution)/shard_map/while/body/eval_jaxpr/all_to_all | solution.py:65
  297.2 2.9 copy-start
  304.0 17.3 %all-to-all-start = ((f32[2,4,128,128]{3,1,0,2:T(4,128)}), f32[2,4,128,128]{3,1,0,2:T(4,128)S(1)}, u32[]{:S(2)}, u32[]{:S(2)}) async-start(f32[2,4,128,128]{3,1,0,2:T(4,128)} %copy.82), calls=%async_computation | async-start | bytes 1048576 | tf_op jit(solution)/shard_map/while/body/eval_jaxpr/all_to_all | solution.py:55
  321.3 14.8 %all-to-all-start.1 = ((f32[2,4,128,128]{3,1,0,2:T(4,128)}), f32[2,4,128,128]{3,1,0,2:T(4,128)S(1)}, u32[]{:S(2)}, u32[]{:S(2)}) async-start(f32[2,4,128,128]{3,1,0,2:T(4,128)} %copy.85), calls=%async_computation.1 | async-start | bytes 1048576 | tf_op jit(solution)/shard_map/while/body/eval_jaxpr/all_to_all | solution.py:56
  343.7 15.1 %all-to-all-start.2 = ((f32[2,128,4,128]{3,2,0,1:T(4,128)}), f32[2,128,4,128]{3,2,0,1:T(4,128)S(1)}, u32[]{:S(2)}, u32[]{:S(2)}) async-start(f32[2,128,4,128]{3,2,0,1:T(4,128)} %copy.88), calls=%async_computation.2 | async-start | bytes 1048576 | tf_op jit(solution)/shard_map/while/body/eval_jaxpr/all_to_all | solution.py:64
  358.8 14.8 %all-to-all-start.3 = ((f32[2,128,4,128]{3,2,0,1:T(4,128)}), f32[2,128,4,128]{3,2,0,1:T(4,128)S(1)}, u32[]{:S(2)}, u32[]{:S(2)}) async-start(f32[2,128,4,128]{3,2,0,1:T(4,128)} %copy.91), calls=%async_computation.3 | async-start | bytes 1048576 | tf_op jit(solution)/shard_map/while/body/eval_jaxpr/all_to_all | solution.py:65
  381.0 2.9 copy-start
  387.8 14.8 %all-to-all-start = ((f32[2,4,128,128]{3,1,0,2:T(4,128)}), f32[2,4,128,128]{3,1,0,2:T(4,128)S(1)}, u32[]{:S(2)}, u32[]{:S(2)}) async-start(f32[2,4,128,128]{3,1,0,2:T(4,128)} %copy.82), calls=%async_computation | async-start | bytes 1048576 | tf_op jit(solution)/shard_map/while/body/eval_jaxpr/all_to_all | solution.py:55
  402.5 15.6 %all-to-all-start.1 = ((f32[2,4,128,128]{3,1,0,2:T(4,128)}), f32[2,4,128,128]{3,1,0,2:T(4,128)S(1)}, u32[]{:S(2)}, u32[]{:S(2)}) async-start(f32[2,4,128,128]{3,1,0,2:T(4,128)} %copy.85), calls=%async_computation.1 | async-start | bytes 1048576 | tf_op jit(solution)/shard_map/while/body/eval_jaxpr/all_to_all | solution.py:56
  425.8 14.8 %all-to-all-start.2 = ((f32[2,128,4,128]{3,2,0,1:T(4,128)}), f32[2,128,4,128]{3,2,0,1:T(4,128)S(1)}, u32[]{:S(2)}, u32[]{:S(2)}) async-start(f32[2,128,4,128]{3,2,0,1:T(4,128)} %copy.88), calls=%async_computation.2 | async-start | bytes 1048576 | tf_op jit(solution)/shard_map/while/body/eval_jaxpr/all_to_all | solution.py:64
  440.6 14.8 %all-to-all-start.3 = ((f32[2,128,4,128]{3,2,0,1:T(4,128)}), f32[2,128,4,128]{3,2,0,1:T(4,128)S(1)}, u32[]{:S(2)}, u32[]{:S(2)}) async-start(f32[2,128,4,128]{3,2,0,1:T(4,128)} %copy.91), calls=%async_computation.3 | async-start | bytes 1048576 | tf_op jit(solution)/shard_map/while/body/eval_jaxpr/all_to_all | solution.py:65
  462.9 2.9 copy-start
  469.6 14.8 %all-to-all-start = ((f32[2,4,128,128]{3,1,0,2:T(4,128)}), f32[2,4,128,128]{3,1,0,2:T(4,128)S(1)}, u32[]{:S(2)}, u32[]{:S(2)}) async-start(f32[2,4,128,128]{3,1,0,2:T(4,128)} %copy.82), calls=%async_computation | async-start | bytes 1048576 | tf_op jit(solution)/shard_map/while/body/eval_jaxpr/all_to_all | solution.py:55
  484.4 14.9 %all-to-all-start.1 = ((f32[2,4,128,128]{3,1,0,2:T(4,128)}), f32[2,4,128,128]{3,1,0,2:T(4,128)S(1)}, u32[]{:S(2)}, u32[]{:S(2)}) async-start(f32[2,4,128,128]{3,1,0,2:T(4,128)} %copy.85), calls=%async_computation.1 | async-start | bytes 1048576 | tf_op jit(solution)/shard_map/while/body/eval_jaxpr/all_to_all | solution.py:56
  507.0 14.8 %all-to-all-start.2 = ((f32[2,128,4,128]{3,2,0,1:T(4,128)}), f32[2,128,4,128]{3,2,0,1:T(4,128)S(1)}, u32[]{:S(2)}, u32[]{:S(2)}) async-start(f32[2,128,4,128]{3,2,0,1:T(4,128)} %copy.88), calls=%async_computation.2 | async-start | bytes 1048576 | tf_op jit(solution)/shard_map/while/body/eval_jaxpr/all_to_all | solution.py:64
  521.8 16.0 %all-to-all-start.3 = ((f32[2,128,4,128]{3,2,0,1:T(4,128)}), f32[2,128,4,128]{3,2,0,1:T(4,128)S(1)}, u32[]{:S(2)}, u32[]{:S(2)}) async-start(f32[2,128,4,128]{3,2,0,1:T(4,128)} %copy.91), calls=%async_computation.3 | async-start | bytes 1048576 | tf_op jit(solution)/shard_map/while/body/eval_jaxpr/all_to_all | solution.py:65
  545.3 2.9 copy-start
  552.0 14.7 %all-to-all-start = ((f32[2,4,128,128]{3,1,0,2:T(4,128)}), f32[2,4,128,128]{3,1,0,2:T(4,128)S(1)}, u32[]{:S(2)}, u32[]{:S(2)}) async-start(f32[2,4,128,128]{3,1,0,2:T(4,128)} %copy.82), calls=%async_computation | async-start | bytes 1048576 | tf_op jit(solution)/shard_map/while/body/eval_jaxpr/all_to_all | solution.py:55
  566.7 14.9 %all-to-all-start.1 = ((f32[2,4,128,128]{3,1,0,2:T(4,128)}), f32[2,4,128,128]{3,1,0,2:T(4,128)S(1)}, u32[]{:S(2)}, u32[]{:S(2)}) async-start(f32[2,4,128,128]{3,1,0,2:T(4,128)} %copy.85), calls=%async_computation.1 | async-start | bytes 1048576 | tf_op jit(solution)/shard_map/while/body/eval_jaxpr/all_to_all | solution.py:56
  589.3 14.7 %all-to-all-start.2 = ((f32[2,128,4,128]{3,2,0,1:T(4,128)}), f32[2,128,4,128]{3,2,0,1:T(4,128)S(1)}, u32[]{:S(2)}, u32[]{:S(2)}) async-start(f32[2,128,4,128]{3,2,0,1:T(4,128)} %copy.88), calls=%async_computation.2 | async-start | bytes 1048576 | tf_op jit(solution)/shard_map/while/body/eval_jaxpr/all_to_all | solution.py:64
  603.9 14.8 %all-to-all-start.3 = ((f32[2,128,4,128]{3,2,0,1:T(4,128)}), f32[2,128,4,128]{3,2,0,1:T(4,128)S(1)}, u32[]{:S(2)}, u32[]{:S(2)}) async-start(f32[2,128,4,128]{3,2,0,1:T(4,128)} %copy.91), calls=%async_computation.3 | async-start | bytes 1048576 | tf_op jit(solution)/shard_map/while/body/eval_jaxpr/all_to_all | solution.py:65
  626.2 2.9 copy-start
  632.9 15.0 %all-to-all-start = ((f32[2,4,128,128]{3,1,0,2:T(4,128)}), f32[2,4,128,128]{3,1,0,2:T(4,128)S(1)}, u32[]{:S(2)}, u32[]{:S(2)}) async-start(f32[2,4,128,128]{3,1,0,2:T(4,128)} %copy.82), calls=%async_computation | async-start | bytes 1048576 | tf_op jit(solution)/shard_map/while/body/eval_jaxpr/all_to_all | solution.py:55
  647.9 15.6 %all-to-all-start.1 = ((f32[2,4,128,128]{3,1,0,2:T(4,128)}), f32[2,4,128,128]{3,1,0,2:T(4,128)S(1)}, u32[]{:S(2)}, u32[]{:S(2)}) async-start(f32[2,4,128,128]{3,1,0,2:T(4,128)} %copy.85), calls=%async_computation.1 | async-start | bytes 1048576 | tf_op jit(solution)/shard_map/while/body/eval_jaxpr/all_to_all | solution.py:56
  671.1 14.7 %all-to-all-start.2 = ((f32[2,128,4,128]{3,2,0,1:T(4,128)}), f32[2,128,4,128]{3,2,0,1:T(4,128)S(1)}, u32[]{:S(2)}, u32[]{:S(2)}) async-start(f32[2,128,4,128]{3,2,0,1:T(4,128)} %copy.88), calls=%async_computation.2 | async-start | bytes 1048576 | tf_op jit(solution)/shard_map/while/body/eval_jaxpr/all_to_all | solution.py:64
  685.9 14.8 %all-to-all-start.3 = ((f32[2,128,4,128]{3,2,0,1:T(4,128)}), f32[2,128,4,128]{3,2,0,1:T(4,128)S(1)}, u32[]{:S(2)}, u32[]{:S(2)}) async-start(f32[2,128,4,128]{3,2,0,1:T(4,128)} %copy.91), calls=%async_computation.3 | async-start | bytes 1048576 | tf_op jit(solution)/shard_map/while/body/eval_jaxpr/all_to_all | solution.py:65
Sparse Core Ops, SparseCore 0:
  9.2 39.4 all-gather.1
where the time goes:
time: 720 us; the launch traced here: 716 us
  waiting for transfers between devices  311 us (43%)
  matrix products  171 us (24%)
  starting transfers between devices  162 us (22%)
  local copies, waits for them, and re-layouts  55.7 us (8%)
  between operations  13.4 us (2%)
    dot_general x160, matrix products, transform_axis(): return jnp.einsum(pattern, values, matrix, precision=finest)  171 us
    all_to_all x8, waiting for transfers between devices, potentials(): lax.all_to_all(imag_part, 'plane', split_axis=2, concat_axis=1, tiled=True)  77 us
    all_to_all x8, waiting for transfers between devices, potentials(): lax.all_to_all(second, 'plane', split_axis=1, concat_axis=2, tiled=True)  75.7 us
    all_to_all x8, waiting for transfers between devices, potentials(): lax.all_to_all(real_part, 'plane', split_axis=2, concat_axis=1, tiled=True)  59.1 us
    all_to_all x8, waiting for transfers between devices, potentials(): lax.all_to_all(first, 'plane', split_axis=1, concat_axis=2, tiled=True)  57.9 us
    all_to_all x8, starting transfers between devices, potentials(): lax.all_to_all(real_part, 'plane', split_axis=2, concat_axis=1, tiled=True)  42.3 us
    all_gather x1, waiting for transfers between devices, on_device(): everyone = lax.all_gather(sources, 'band', axis=0, tiled=True)  40.3 us
    all_to_all x8, starting transfers between devices, potentials(): lax.all_to_all(second, 'plane', split_axis=1, concat_axis=2, tiled=True)  40 us
  transfers between devices with their start and end apart: 33, of which 33 were waited for; matrix products, arithmetic and copies ran while one was open for 7% of the time, Pallas kernels for 0%

commit v1 on v0

v1 whole, which is shorter than its diff:
```python
import math

import jax
import jax.numpy as jnp
import ml_dtypes
import numpy as np
from jax import lax
from jax.experimental import pallas as pl
from jax.experimental.pallas import tpu as pltpu
from jax.sharding import PartitionSpec as P

exact_share = 0.25
vmem_limit = 48 * 1024 * 1024


def halves(matrix):
    high = matrix.astype(ml_dtypes.bfloat16)
    low = (matrix - high.astype(np.float64)).astype(ml_dtypes.bfloat16)
    return np.stack([high, low])


def dft_matrices(length, planes):
    indices = np.arange(length)
    angles = (indices[:, None] * indices[None, :] % length) * (2.0 * math.pi / length)
    cosine, sine = np.cos(angles), np.sin(angles)
    forward = np.block([[cosine, sine], [-sine, cosine]])
    inverse = np.block([[cosine, -sine], [sine, cosine]])
    order = np.arange(2 * length).reshape(2, length // planes, planes).transpose(1, 0, 2).reshape(-1)
    return (
        halves(forward.T),
        halves(forward),
        halves(forward[:, order]),
        halves(inverse[order, :]),
        halves(inverse),
        halves(inverse.T),
    )


def split(values):
    high = values.astype(jnp.bfloat16)
    low = (values - high.astype(jnp.float32)).astype(jnp.bfloat16)
    return high, low


def dot(left, right):
    return jnp.dot(left, right, preferred_element_type=jnp.float32)


def from_left(matrix_ref, values):
    high, low = split(values)
    return dot(matrix_ref[0], high) + dot(matrix_ref[0], low) + dot(matrix_ref[1], high)


def from_right(values, matrix_ref):
    high, low = split(values)
    return dot(high, matrix_ref[0]) + dot(low, matrix_ref[0]) + dot(high, matrix_ref[1])


def forward_kernel(length, planes, targets_ref, source_ref, z_ref, y_ref, out_ref):
    rows = planes * length
    source = source_ref[...].reshape(rows, length)
    density = jnp.concatenate(
        [targets_ref[part].reshape(rows, length) * source for part in range(2)], axis=1
    )
    along_z = from_right(density, z_ref)
    stacked = jnp.concatenate(
        [
            jnp.concatenate(
                [
                    along_z[p * length : (p + 1) * length, part * length : (part + 1) * length]
                    for part in range(2)
                ],
                axis=0,
            )
            for p in range(planes)
        ],
        axis=1,
    )
    along_y = from_left(y_ref, stacked)
    flat = out_ref.reshape(length * 2 * planes, length)
    for part in range(2):
        for p in range(planes):
            flat[pl.ds(part * planes + p, length, stride=2 * planes), :] = along_y[
                part * length : (part + 1) * length, p * length : (p + 1) * length
            ]


def middle_kernel(length, planes, values_ref, kernel_ref, x_ref, back_ref, out_ref):
    group = 2 * planes
    parts = length // planes
    values = jnp.concatenate(
        [
            values_ref[:, k * group : (k + 1) * group, :].reshape(2 * length, length)
            for k in range(planes)
        ],
        axis=1,
    )
    spectrum = from_left(x_ref, values)
    weight = jnp.concatenate([kernel_ref[k] for k in range(planes)], axis=1)
    weighted = jnp.concatenate([spectrum[:length] * weight, spectrum[length:] * weight], axis=0)
    back = from_left(back_ref, weighted)
    for k in range(planes):
        out_ref[:, k * group : (k + 1) * group, :] = back[
            :, k * length : (k + 1) * length
        ].reshape(parts, group, length)


def backward_kernel(length, planes, scale, values_ref, source_ref, y_ref, z_ref, sum_ref, out_ref):
    rows = planes * length
    flat = values_ref.reshape(length * 2 * planes, length)
    stacked = jnp.concatenate(
        [
            jnp.concatenate(
                [flat[pl.ds(part * planes + p, length, stride=2 * planes), :] for p in range(planes)],
                axis=1,
            )
            for part in range(2)
        ],
        axis=0,
    )
    along_y = from_left(y_ref, stacked)
    unstacked = jnp.concatenate(
        [
            jnp.concatenate(
                [
                    along_y[part * length : (part + 1) * length, p * length : (p + 1) * length]
                    for part in range(2)
                ],
                axis=1,
            )
            for p in range(planes)
        ],
        axis=0,
    )
    potential = from_right(unstacked, z_ref)
    source = source_ref[...].reshape(rows, length) * scale

    @pl.when(pl.program_id(0) == 0)
    def _():
        out_ref[...] = sum_ref[...]

    for part in range(2):
        term = potential[:, part * length : (part + 1) * length] * source
        out_ref[part] += term.reshape(planes, length, length)


def whole(shape):
    return pl.BlockSpec(shape, lambda s: (0,) * len(shape))


def params():
    return pltpu.CompilerParams(vmem_limit_bytes=vmem_limit, dimension_semantics=("arbitrary",))


def cost(count, rows, columns, passes):
    return pl.CostEstimate(
        flops=count * passes * 6 * rows * rows * columns,
        bytes_accessed=count * 3 * 4 * rows * columns,
        transcendentals=0,
    )


def solution(mesh):
    shards = mesh.shape["plane"]

    def on_device(targets, sources, kernel):
        length = targets.shape[-1]
        planes = targets.shape[1]
        group = 2 * planes * planes
        z_fwd, y_fwd, x_fwd, x_bwd, y_bwd, z_bwd = (
            jnp.asarray(m) for m in dft_matrices(length, planes)
        )
        square = (2, 2 * length, 2 * length)
        slab = pl.BlockSpec((None, planes, length, length), lambda s: (s, 0, 0, 0))
        block = pl.BlockSpec((shards, None, group, length), lambda s: (0, s, 0, 0))
        fields = (2, planes, length, length)
        grid_kernel = (kernel * (1.0 / float(length) ** 3)).transpose(1, 0, 2)

        def packed(count):
            return jax.ShapeDtypeStruct((shards, count, group, length), jnp.float32)

        def exchange(values):
            return lax.all_to_all(values, "plane", split_axis=0, concat_axis=0, tiled=True)

        def forward(batch):
            count = batch.shape[0]
            return pl.pallas_call(
                lambda *refs: forward_kernel(length, planes, *refs),
                grid=(count,),
                in_specs=[whole(fields), slab, whole(square), whole(square)],
                out_specs=block,
                out_shape=packed(count),
                compiler_params=params(),
                cost_estimate=cost(count, 2 * length, planes * length, 2),
                name="forward",
            )(targets, batch, z_fwd, y_fwd)

        def middle(values):
            count = values.shape[1]
            return pl.pallas_call(
                lambda *refs: middle_kernel(length, planes, *refs),
                grid=(count,),
                in_specs=[block, whole((planes, length, length)), whole(square), whole(square)],
                out_specs=block,
                out_shape=packed(count),
                compiler_params=params(),
                cost_estimate=cost(count, 2 * length, planes * length, 2),
                name="middle",
            )(values, grid_kernel, x_fwd, x_bwd)

        def backward(values, batch, summed):
            count = values.shape[1]
            return pl.pallas_call(
                lambda *refs: backward_kernel(length, planes, -exact_share, *refs),
                grid=(count,),
                in_specs=[block, slab, whole(square), whole(square), whole(fields)],
                out_specs=whole(fields),
                out_shape=jax.ShapeDtypeStruct(fields, jnp.float32),
                compiler_params=params(),
                cost_estimate=cost(count, 2 * length, planes * length, 2),
                name="backward",
            )(values, batch, y_bwd, z_bwd, summed)

        everyone = lax.all_gather(sources, "band", axis=0, tiled=True)
        half = everyone.shape[0] // 2
        batches = [everyone[:half], everyone[half:]]
        there = [exchange(forward(batch)) for batch in batches]
        here = [exchange(middle(values)) for values in there]
        summed = jnp.zeros_like(targets)
        for values, batch in zip(here, batches):
            summed = backward(values, batch, summed)
        return summed

    return jax.shard_map(
        on_device,
        mesh=mesh,
        in_specs=(
            P("band", "plane", None, None),
            P("band", "plane", None, None),
            P(None, "plane", None),
        ),
        out_specs=P("band", "plane", None, None),
        check_vma=False,
    )
```

time: 720 us -> 218 us (0.30)
  waiting for transfers between devices: 311 us -> 129 us
  matrix products: 171 us -> 0 us
  starting transfers between devices: 162 us -> 23.1 us
  local copies, waits for them, and re-layouts: 55.7 us -> 24.7 us
  Pallas kernels: 0 us -> 24.1 us
    all_to_all x32 -> x4, waiting for transfers between devices: 270 us -> 86.5 us  [exchange(): lax.all_to_all(values, 'plane', split_axis=0, concat_axis=0, tiled=True)]
    dot_general x160 -> x0, matrix products: 171 us -> none  [transform_axis(): return jnp.einsum(pattern, values, matrix, precision=finest)]
    all_to_all x32 -> x4, starting transfers between devices: 162 us -> 23.1 us  [exchange(): lax.all_to_all(values, 'plane', split_axis=0, concat_axis=0, tiled=True)]
    pallas_call x0 -> x6, Pallas kernels: none -> 24.1 us  [the longest x2 9.05 us: backward(): pl.pallas_call(lambda *refs: backward_kernel(length, planes, -exact_share...]
    unnamed x1 -> x48, local copies, waits for them, and re-layouts: 1.07 us -> 23 us
    add x16 -> x0, local copies, waits for them, and re-layouts: 16.1 us -> none  [the longest x8 8.11 us: inverse(): transform_axis(imag_part, pattern, cosine_table)]
    sub x16 -> x0, local copies, waits for them, and re-layouts: 16.1 us -> none  [the longest x8 8.11 us: forward(): transform_axis(imag_part, pattern, cosine_table)]
    all_to_all x64 -> x0, local copies, waits for them, and re-layouts: 14.2 us -> none  [the longest x16 3.55 us: potentials(): lax.all_to_all(first, 'plane', split_axis=1, concat_axis=2, tiled=True)]
  transfers between devices with their start and end apart: 33 -> 5, of which waited for: 33 -> 5; matrix products, arithmetic and copies ran while one was open for 7% -> 0% of each run, Pallas kernels for 0% -> 7%
where the time goes in v1:
time: 218 us; the launch traced here: 215 us
  waiting for transfers between devices  129 us (59%)
  local copies, waits for them, and re-layouts  24.7 us (11%)
  Pallas kernels  24.1 us (11%)
  starting transfers between devices  23.1 us (11%)
  between operations  13.6 us (6%)
    all_to_all x4, waiting for transfers between devices, exchange(): lax.all_to_all(values, 'plane', split_axis=0, concat_axis=0, tiled=True)  86.5 us
    all_gather x1, waiting for transfers between devices, on_device(): everyone = lax.all_gather(sources, 'band', axis=0, tiled=True)  41.4 us
    all_to_all x4, starting transfers between devices, exchange(): lax.all_to_all(values, 'plane', split_axis=0, concat_axis=0, tiled=True)  23.1 us
    unnamed x48, local copies, waits for them, and re-layouts  23 us
    pallas_call x2, Pallas kernels, backward(): pl.pallas_call(lambda *refs: backward_kernel(length, planes, -exact_share...  9.05 us
    pallas_call x2, Pallas kernels, forward(): pl.pallas_call(lambda *refs: forward_kernel(length, planes, *refs), grid=...  8.5 us
    pallas_call x2, Pallas kernels, middle(): pl.pallas_call(lambda *refs: middle_kernel(length, planes, *refs), grid=(...  6.56 us
  transfers between devices with their start and end apart: 5, of which 5 were waited for; matrix products, arithmetic and copies ran while one was open for 0% of the time, Pallas kernels for 7%

profile of v1, /device:TPU:8, one launch (start us, length us, event | category | flops | bytes accessed | tf_op | source)
XLA Modules:
  0.0 215.1 jit_solution(18233260159857070519)
XLA Ops:
  6.5 0.0 all-gather.2.cloned.1.call-start
  6.5 0.7 all-gather.2.cloned.1.call-update
  7.3 0.0 copy-start.10
  7.3 0.0 copy-start.12
  7.3 0.0 copy-start.14
  7.3 41.4 %all-gather.2.cloned.1.call-done = f32[8,4,128,128]{3,2,1,0:T(8,128)} async-done(((f32[1,4,128,128]{3,2,1,0:T(8,128)}), f32[8,4,128,128]{3,2,1,0:T(8,128)}) %all-gather.2.cloned.1.call-update) | async-done | bytes 2097168 | tf_op jit(solution)/shard_map/all_gather | solution.py:224
  48.7 1.7 fusion.1
  50.4 0.0 copy-done.10
  50.4 0.0 copy-done.12
  50.4 0.0 copy-done.14
  50.4 4.3 %forward.3 = f32[32,4,32,128]{3,2,1,0:T(8,128)S(1)} custom-call(f32[2,4,128,128]{3,2,1,0:T(8,128)S(1)} %copy-done.10, f32[4,4,128,128]{3,2,1,0:T(8,128)S(1)} %get-tuple-element.5.refs_1_, bf16[2,256,256]{2,1,0:T(8,128)(2,1)S(1)} %copy-done.12, bf16[2,256,256]{2,1,0:T(8,128)(2,1)S(1)} %copy-done.14), custom_call_target="tpu_custom_call" | custom-call | flops 1610612736 | bytes 6291456 | tf_op jit(solution)/shard_map/forward/pallas_call | solution.py:187
  54.7 0.0 copy-start.7
  54.7 1.3 copy-done.7
  56.0 0.0 copy-start.8
  56.0 1.0 copy-done.8
  57.1 7.4 %all-to-all-start.2 = ((f32[32,4,32,128]{3,2,1,0:T(8,128)}), f32[32,4,32,128]{3,2,1,0:T(8,128)S(1)}, u32[]{:S(2)}, u32[]{:S(2)}) async-start(f32[32,4,32,128]{3,2,1,0:T(8,128)} %copy-done.7), calls=%async_computation.2 | async-start | bytes 4194304 | tf_op jit(solution)/shard_map/all_to_all | solution.py:183
  64.5 0.0 copy-start.11
  64.5 1.0 copy-done.11
  65.5 0.9 copy-done.15
  66.5 4.2 %forward.2 = f32[32,4,32,128]{3,2,1,0:T(8,128)S(1)} custom-call(f32[2,4,128,128]{3,2,1,0:T(8,128)S(1)} %copy-done.11, f32[4,4,128,128]{3,2,1,0:T(8,128)S(1)} %get-tuple-element.6.refs_1_, bf16[2,256,256]{2,1,0:T(8,128)(2,1)S(1)} %copy-done.12, bf16[2,256,256]{2,1,0:T(8,128)(2,1)S(1)} %copy-done.15), custom_call_target="tpu_custom_call" | custom-call | flops 1610612736 | bytes 6291456 | tf_op jit(solution)/shard_map/forward/pallas_call | solution.py:187
  70.7 0.0 copy-start.6
  70.7 1.3 copy-done.6
  72.1 23.4 %all-to-all-done.2.refs_0_ = f32[32,4,32,128]{3,2,1,0:T(8,128)S(1)} async-done(((f32[32,4,32,128]{3,2,1,0:T(8,128)}), f32[32,4,32,128]{3,2,1,0:T(8,128)S(1)}, u32[]{:S(2)}, u32[]{:S(2)}) %all-to-all-start.2) | async-done | bytes 2097184 | tf_op jit(solution)/shard_map/all_to_all | solution.py:183
  95.5 0.0 copy-start.3
  95.5 1.3 copy-done.3
  96.8 6.5 %all-to-all-start = ((f32[32,4,32,128]{3,2,1,0:T(8,128)}), f32[32,4,32,128]{3,2,1,0:T(8,128)S(1)}, u32[]{:S(2)}, u32[]{:S(2)}) async-start(f32[32,4,32,128]{3,2,1,0:T(8,128)} %copy-done.6), calls=%async_computation | async-start | bytes 4194304 | tf_op jit(solution)/shard_map/all_to_all | solution.py:183
  103.3 1.0 fusion.refs_1_
  104.3 0.0 copy-start.4
  104.3 1.6 copy-done.4
  105.9 0.0 copy-start.18
  105.9 0.9 copy-done.18
  106.8 0.0 copy-start.20
  106.8 0.9 copy-done.20
  107.8 3.3 %middle.3 = f32[32,4,32,128]{3,2,1,0:T(8,128)S(1)} custom-call(f32[32,4,32,128]{3,2,1,0:T(8,128)S(1)} %copy-done.4, f32[4,128,128]{2,1,0:T(8,128)S(1)} %fusion.refs_1_, bf16[2,256,256]{2,1,0:T(8,128)(2,1)S(1)} %copy-done.18, bf16[2,256,256]{2,1,0:T(8,128)(2,1)S(1)} %copy-done.20), custom_call_target="tpu_custom_call" | custom-call | flops 1610612736 | bytes 6291456 | tf_op jit(solution)/shard_map/middle/pallas_call | solution.py:200
  111.1 0.0 copy-start.5
  111.1 1.3 copy-done.5
  112.4 22.0 %all-to-all-done.refs_0_ = f32[32,4,32,128]{3,2,1,0:T(8,128)S(1)} async-done(((f32[32,4,32,128]{3,2,1,0:T(8,128)}), f32[32,4,32,128]{3,2,1,0:T(8,128)S(1)}, u32[]{:S(2)}, u32[]{:S(2)}) %all-to-all-start) | async-done | bytes 2097184 | tf_op jit(solution)/shard_map/all_to_all | solution.py:183
  134.4 0.0 copy-start
  134.4 1.3 copy-done
  135.7 4.6 %all-to-all-start.3 = ((f32[32,4,32,128]{3,2,1,0:T(8,128)}), f32[32,4,32,128]{3,2,1,0:T(8,128)S(1)}, u32[]{:S(2)}, u32[]{:S(2)}) async-start(f32[32,4,32,128]{3,2,1,0:T(8,128)} %copy-done.5), calls=%async_computation.3 | async-start | bytes 4194304 | tf_op jit(solution)/shard_map/all_to_all | solution.py:183
  140.3 0.0 copy-start.1
  140.3 1.6 copy-done.1
  141.9 0.0 copy-start.19
  141.9 0.9 copy-done.19
  142.9 0.0 copy-start.21
  142.9 0.9 copy-done.21
  143.8 3.3 %middle.2 = f32[32,4,32,128]{3,2,1,0:T(8,128)S(1)} custom-call(f32[32,4,32,128]{3,2,1,0:T(8,128)S(1)} %copy-done.1, f32[4,128,128]{2,1,0:T(8,128)S(1)} %fusion.refs_1_, bf16[2,256,256]{2,1,0:T(8,128)(2,1)S(1)} %copy-done.19, bf16[2,256,256]{2,1,0:T(8,128)(2,1)S(1)} %copy-done.21), custom_call_target="tpu_custom_call" | custom-call | flops 1610612736 | bytes 6291456 | tf_op jit(solution)/shard_map/middle/pallas_call | solution.py:200
  147.1 0.0 copy-start.2
  147.1 1.3 copy-done.2
  148.5 0.0 copy-start.13
  148.5 21.2 %all-to-all-done.3.refs_0_ = f32[32,4,32,128]{3,2,1,0:T(8,128)S(1)} async-done(((f32[32,4,32,128]{3,2,1,0:T(8,128)}), f32[32,4,32,128]{3,2,1,0:T(8,128)S(1)}, u32[]{:S(2)}, u32[]{:S(2)}) %all-to-all-start.3) | async-done | bytes 2097184 | tf_op jit(solution)/shard_map/all_to_all | solution.py:183
  169.7 4.6 %all-to-all-start.1 = ((f32[32,4,32,128]{3,2,1,0:T(8,128)}), f32[32,4,32,128]{3,2,1,0:T(8,128)}, u32[]{:S(2)}, u32[]{:S(2)}) async-start(f32[32,4,32,128]{3,2,1,0:T(8,128)} %copy-done.2), calls=%async_computation.1 | async-start | bytes 4194304 | tf_op jit(solution)/shard_map/all_to_all | solution.py:183
  174.4 0.0 copy-done.13
  174.4 0.0 copy-start.9
  174.4 1.2 copy-done.9
  175.6 0.0 copy-start.16
  175.6 0.9 copy-done.16
  176.6 3.5 %backward.2.refs_4_ = f32[2,4,128,128]{3,2,1,0:T(8,128)S(1)} custom-call(f32[32,4,32,128]{3,2,1,0:T(8,128)S(1)} %all-to-all-done.3.refs_0_, f32[4,4,128,128]{3,2,1,0:T(8,128)S(1)} %copy-done.9, bf16[2,256,256]{2,1,0:T(8,128)(2,1)S(1)} %copy-done.13, bf16[2,256,256]{2,1,0:T(8,128)(2,1)S(1)} %copy-done.16, f32[2,4,128,128]{3,2,1,0:T(8,128)S(1)} %broadcast_in_dim.3.refs_4_), custom_call_target="tpu_custom_call" | custom-call | flops 1610612736 | bytes 6291456 | tf_op jit(solution)/shard_map/backward/pallas_call | solution.py:213
  180.1 0.0 copy-start.22
  180.1 0.8 copy-done.22
  180.9 19.8 %all-to-all-done.1.refs_0_ = f32[32,4,32,128]{3,2,1,0:T(8,128)} async-done(((f32[32,4,32,128]{3,2,1,0:T(8,128)}), f32[32,4,32,128]{3,2,1,0:T(8,128)}, u32[]{:S(2)}, u32[]{:S(2)}) %all-to-all-start.1) | async-done | bytes 2097184 | tf_op jit(solution)/shard_map/all_to_all | solution.py:183
  200.7 0.9 copy-done.17
  201.7 1.0 copy-done.23
  202.7 5.5 %backward.3 = f32[2,4,128,128]{3,2,1,0:T(8,128)} custom-call(f32[32,4,32,128]{3,2,1,0:T(8,128)} %all-to-all-done.1.refs_0_, f32[4,4,128,128]{3,2,1,0:T(8,128)S(1)} %get-tuple-element.6.refs_1_, bf16[2,256,256]{2,1,0:T(8,128)(2,1)S(1)} %copy-done.13, bf16[2,256,256]{2,1,0:T(8,128)(2,1)S(1)} %copy-done.17, f32[2,4,128,128]{3,2,1,0:T(8,128)S(1)} %copy-done.23), custom_call_target="tpu_custom_call" | custom-call | flops 1610612736 | bytes 6291456 | tf_op jit(solution)/shard_map/backward/pallas_call | solution.py:213
  (4 shorter events, 0.0 us)
Async XLA Ops:
  6.5 42.1 %all-gather.2.cloned.1.call-start = ((), (), s32[]{:S(2)}) async-start(), calls=%async_computation.4 | async-start | bytes 2359296 | tf_op jit(solution)/shard_map/all_gather | solution.py:224
  7.3 43.1 %copy-start.10 = (f32[2,4,128,128]{3,2,1,0:T(8,128)S(1)}, f32[2,4,128,128]{3,2,1,0:T(8,128)}, u32[]{:S(2)}) copy-start(f32[2,4,128,128]{3,2,1,0:T(8,128)} %refs_0_.3) | copy-start | bytes 1572868
  7.3 43.1 %copy-start.12 = (bf16[2,256,256]{2,1,0:T(8,128)(2,1)S(1)}, bf16[2,256,256]{2,1,0:T(8,128)(2,1)}, u32[]{:S(2)}) copy-start(bf16[2,256,256]{2,1,0:T(8,128)(2,1)} %constant.12.clone.refs_2_) | copy-start | bytes 786436
  7.3 43.1 %copy-start.14 = (bf16[2,256,256]{2,1,0:T(8,128)(2,1)S(1)}, bf16[2,256,256]{2,1,0:T(8,128)(2,1)}, u32[]{:S(2)}) copy-start(bf16[2,256,256]{2,1,0:T(8,128)(2,1)} %constant.13.clone.refs_3_) | copy-start | bytes 786436
  54.7 1.3 copy-start.7
  56.0 1.0 copy-start.8
  57.1 38.4 %all-to-all-start.2 = ((f32[32,4,32,128]{3,2,1,0:T(8,128)}), f32[32,4,32,128]{3,2,1,0:T(8,128)S(1)}, u32[]{:S(2)}, u32[]{:S(2)}) async-start(f32[32,4,32,128]{3,2,1,0:T(8,128)} %copy-done.7), calls=%async_computation.2 | async-start | bytes 4194304 | tf_op jit(solution)/shard_map/all_to_all | solution.py:183
  64.5 1.0 copy-start.11
  65.5 0.9 copy-start.15
  70.7 1.3 copy-start.6
  95.5 1.3 copy-start.3
  96.8 37.6 %all-to-all-start = ((f32[32,4,32,128]{3,2,1,0:T(8,128)}), f32[32,4,32,128]{3,2,1,0:T(8,128)S(1)}, u32[]{:S(2)}, u32[]{:S(2)}) async-start(f32[32,4,32,128]{3,2,1,0:T(8,128)} %copy-done.6), calls=%async_computation | async-start | bytes 4194304 | tf_op jit(solution)/shard_map/all_to_all | solution.py:183
  104.3 1.6 copy-start.4
  105.9 0.9 copy-start.18
  106.8 0.9 copy-start.20
  111.1 1.3 copy-start.5
  134.4 1.3 copy-start
  135.7 33.9 %all-to-all-start.3 = ((f32[32,4,32,128]{3,2,1,0:T(8,128)}), f32[32,4,32,128]{3,2,1,0:T(8,128)S(1)}, u32[]{:S(2)}, u32[]{:S(2)}) async-start(f32[32,4,32,128]{3,2,1,0:T(8,128)} %copy-done.5), calls=%async_computation.3 | async-start | bytes 4194304 | tf_op jit(solution)/shard_map/all_to_all | solution.py:183
  140.3 1.6 copy-start.1
  141.9 0.9 copy-start.19
  142.9 0.9 copy-start.21
  147.1 1.3 copy-start.2
  148.5 25.9 %copy-start.13 = (bf16[2,256,256]{2,1,0:T(8,128)(2,1)S(1)}, bf16[2,256,256]{2,1,0:T(8,128)(2,1)}, u32[]{:S(2)}) copy-start(bf16[2,256,256]{2,1,0:T(8,128)(2,1)} %constant.12.clone.refs_2_) | copy-start | bytes 786436
  169.7 31.1 %all-to-all-start.1 = ((f32[32,4,32,128]{3,2,1,0:T(8,128)}), f32[32,4,32,128]{3,2,1,0:T(8,128)}, u32[]{:S(2)}, u32[]{:S(2)}) async-start(f32[32,4,32,128]{3,2,1,0:T(8,128)} %copy-done.2), calls=%async_computation.1 | async-start | bytes 4194304 | tf_op jit(solution)/shard_map/all_to_all | solution.py:183
  174.4 1.2 copy-start.9
  175.6 0.9 copy-start.16
  180.1 0.8 copy-start.22
  200.7 1.0 copy-start.17
  201.7 1.0 copy-start.23
Sparse Core Ops, SparseCore 0:
  9.2 39.4 all-gather.1

commit v2 on v0

v2 whole, which is shorter than its diff:
```python
import math

import jax
import jax.numpy as jnp
import ml_dtypes
import numpy as np
from jax import lax
from jax.experimental import pallas as pl
from jax.experimental.pallas import tpu as pltpu
from jax.sharding import PartitionSpec as P

exact_share = 0.25
vmem_limit = 64 * 1024 * 1024


def halves(matrix):
    high = matrix.astype(ml_dtypes.bfloat16)
    low = (matrix - high.astype(np.float64)).astype(ml_dtypes.bfloat16)
    return high, low


def left_form(matrix):
    high, low = halves(matrix)
    return np.concatenate([high, high, low], axis=1)


def right_form(matrix):
    high, low = halves(matrix)
    return np.concatenate([high, high, low], axis=0)


def dft_matrices(length, planes):
    indices = np.arange(length)
    angles = (indices[:, None] * indices[None, :] % length) * (2.0 * math.pi / length)
    cosine, sine = np.cos(angles), np.sin(angles)
    forward = np.block([[cosine, sine], [-sine, cosine]])
    inverse = np.block([[cosine, -sine], [sine, cosine]])
    order = np.arange(2 * length).reshape(2, length // planes, planes).transpose(1, 0, 2).reshape(-1)
    return (
        (right_form(forward.T), left_form(forward)),
        (left_form(forward[:, order]), left_form(inverse[order, :])),
        (left_form(inverse), right_form(inverse.T)),
    )


def split(values):
    high = values.astype(jnp.bfloat16)
    low = (values - high.astype(jnp.float32)).astype(jnp.bfloat16)
    return high, low


def from_left(matrix_ref, values):
    high, low = split(values)
    stack = jnp.concatenate([high, low, high], axis=0)
    return jnp.dot(matrix_ref[...], stack, preferred_element_type=jnp.float32)


def from_right(values, matrix_ref):
    high, low = split(values)
    stack = jnp.concatenate([high, low, high], axis=1)
    return jnp.dot(stack, matrix_ref[...], preferred_element_type=jnp.float32)


def fetch(pairs, sems):
    copies = [
        pltpu.make_async_copy(source, target, sems.at[i]) for i, (source, target) in enumerate(pairs)
    ]
    for copy in copies:
        copy.start()
    return copies


def turn(values, length, count):
    return jnp.concatenate(
        [
            jnp.concatenate(
                [
                    values[p * length : (p + 1) * length, part * length : (part + 1) * length]
                    for part in range(2)
                ],
                axis=0,
            )
            for p in range(count)
        ],
        axis=1,
    )


def turn_back(values, length, count):
    return jnp.concatenate(
        [
            jnp.concatenate(
                [
                    values[part * length : (part + 1) * length, p * length : (p + 1) * length]
                    for part in range(2)
                ],
                axis=1,
            )
            for p in range(count)
        ],
        axis=0,
    )


def forward_kernel(length, planes, count, bounds_ref, targets_hbm, z_hbm, y_hbm, *refs):
    sources_hbm = refs[:count]
    out_hbm, targets_ref, z_ref, y_ref, sources_ref, out_ref, in_sems, source_sems, out_sems = refs[-9:]
    low, high = bounds_ref[0], bounds_ref[1]
    rows = planes * length
    items = 2 * planes

    def source_copy(i):
        return pltpu.make_async_copy(sources_hbm[i].at[0], sources_ref.at[i], source_sems.at[i])

    def out_copy(i):
        return pltpu.make_async_copy(out_ref.at[i], out_hbm.at[:, i], out_sems.at[i])

    @pl.when(low < high)
    def _():
        fixed = fetch([(targets_hbm, targets_ref), (z_hbm, z_ref), (y_hbm, y_ref)], in_sems)
        for i in range(count):

            @pl.when((low <= i) & (i < high))
            def _(i=i):
                source_copy(i).start()

        for copy in fixed:
            copy.wait()

        def step(n, carry):
            these = [2 * n, 2 * n + 1]
            for i in these:
                pltpu.make_async_copy(
                    sources_hbm[0].at[0], sources_ref.at[i], source_sems.at[i]
                ).wait()
            density = jnp.concatenate(
                [
                    jnp.concatenate(
                        [
                            (targets_ref[part] * sources_ref[i]).reshape(rows, length)
                            for part in range(2)
                        ],
                        axis=1,
                    )
                    for i in these
                ],
                axis=0,
            )
            along_y = from_left(y_ref, turn(from_right(density, z_ref), length, items))
            for at, i in enumerate(these):
                flat = out_ref.at[i].reshape(length * 2 * planes, length)
                for part in range(2):
                    for p in range(planes):
                        item = at * planes + p
                        flat[pl.ds(part * planes + p, length, stride=2 * planes), :] = along_y[
                            part * length : (part + 1) * length, item * length : (item + 1) * length
                        ]
                out_copy(i).start()
            return carry

        lax.fori_loop(low // 2, high // 2, step, 0)
        for i in range(count):

            @pl.when((low <= i) & (i < high))
            def _(i=i):
                out_copy(i).wait()


def middle_kernel(length, planes, count, *refs):
    values_hbm, kernel_hbm, there_hbm, back_hbm, out_hbm = refs[:5]
    values_ref, kernel_ref, there_ref, back_ref, out_ref, in_sems, value_sems, out_sems = refs[5:]
    group = 2 * planes
    parts = length // planes
    fixed = fetch(
        [(kernel_hbm, kernel_ref), (there_hbm, there_ref), (back_hbm, back_ref)], in_sems
    )
    fetch([(values_hbm.at[:, i], values_ref.at[i]) for i in range(count)], value_sems)
    for copy in fixed:
        copy.wait()

    def out_copy(i):
        return pltpu.make_async_copy(out_ref.at[i], out_hbm.at[:, i], out_sems.at[i])

    def step(n, carry):
        these = [2 * n, 2 * n + 1]
        for i in these:
            pltpu.make_async_copy(values_hbm.at[:, i], values_ref.at[i], value_sems.at[i]).wait()
        items = [(i, k) for i in these for k in range(planes)]
        values = jnp.concatenate(
            [
                values_ref[i, :, k * group : (k + 1) * group, :].reshape(2 * length, length)
                for i, k in items
            ],
            axis=1,
        )
        spectrum = from_left(there_ref, values)
        weight = jnp.concatenate([kernel_ref[k] for i, k in items], axis=1)
        weighted = jnp.concatenate([spectrum[:length] * weight, spectrum[length:] * weight], axis=0)
        back = from_left(back_ref, weighted)
        for at, (i, k) in enumerate(items):
            out_ref[i, :, k * group : (k + 1) * group, :] = back[
                :, at * length : (at + 1) * length
            ].reshape(parts, group, length)
        for i in these:
            out_copy(i).start()
        return carry

    lax.fori_loop(0, count // 2, step, 0)
    for i in range(count):
        out_copy(i).wait()


def backward_kernel(length, planes, scale, count, *refs):
    values_hbm, y_hbm, z_hbm, *sources_hbm = refs[: 3 + count]
    out_hbm, values_ref, y_ref, z_ref, sources_ref, out_ref, in_sems, value_sems, source_sems = refs[
        3 + count :
    ]
    rows = planes * length
    fixed = fetch([(y_hbm, y_ref), (z_hbm, z_ref)], in_sems)
    for i, source in enumerate(sources_hbm):
        pltpu.make_async_copy(values_hbm.at[:, i], values_ref.at[i], value_sems.at[i]).start()
        pltpu.make_async_copy(source.at[0], sources_ref.at[i], source_sems.at[i]).start()
    out_ref[...] = jnp.zeros_like(out_ref)
    for copy in fixed:
        copy.wait()

    def step(n, carry):
        these = [2 * n, 2 * n + 1]
        for i in these:
            pltpu.make_async_copy(values_hbm.at[:, i], values_ref.at[i], value_sems.at[i]).wait()
            pltpu.make_async_copy(sources_hbm[0].at[0], sources_ref.at[i], source_sems.at[i]).wait()
        flats = [values_ref.at[i].reshape(length * 2 * planes, length) for i in these]
        stacked = jnp.concatenate(
            [
                jnp.concatenate(
                    [
                        flat[pl.ds(part * planes + p, length, stride=2 * planes), :]
                        for flat in flats
                        for p in range(planes)
                    ],
                    axis=1,
                )
                for part in range(2)
            ],
            axis=0,
        )
        along_y = turn_back(from_left(y_ref, stacked), length, 2 * planes)
        potential = from_right(along_y, z_ref)
        for part in range(2):
            total = out_ref[part].reshape(rows, length)
            for at, i in enumerate(these):
                total += (
                    potential[at * rows : (at + 1) * rows, part * length : (part + 1) * length]
                    * (sources_ref[i].reshape(rows, length) * scale)
                )
            out_ref[part] = total.reshape(planes, length, length)
        return carry

    lax.fori_loop(0, count // 2, step, 0)
    copy = pltpu.make_async_copy(out_ref, out_hbm, in_sems.at[0])
    copy.start()
    copy.wait()


def cost(count, rows, columns):
    return pl.CostEstimate(
        flops=count * 12 * rows * rows * columns,
        bytes_accessed=count * 12 * rows * columns,
        transcendentals=0,
    )


def solution(mesh):
    shards = mesh.shape["plane"]
    bands = mesh.shape["band"]
    swap = [(b, b ^ 1) for b in range(bands)]
    up = [(b, (b + 2) % bands) for b in range(bands)]
    down = [(b, (b - 2) % bands) for b in range(bands)]
    opposite = [(b, (b + 4) % bands) for b in range(bands)]

    def on_device(targets, sources, kernel):
        length = targets.shape[-1]
        planes = targets.shape[1]
        group = 2 * planes * planes
        forward_matrices, middle_matrices, backward_matrices = (
            (jnp.asarray(first), jnp.asarray(second)) for first, second in dft_matrices(length, planes)
        )
        slab = (planes, length, length)
        fields = (2,) + slab
        packed = (shards, group, length)
        left = pltpu.VMEM((2 * length, 6 * length), jnp.bfloat16)
        right = pltpu.VMEM((6 * length, 2 * length), jnp.bfloat16)
        grid_kernel = (kernel * (1.0 / float(length) ** 3)).transpose(1, 0, 2)

        def call(body, name, count, operands, out_shape, scratch, scalars=0, aliases={}):
            return pl.pallas_call(
                lambda *refs: body(*refs),
                in_specs=[pl.BlockSpec(memory_space=pltpu.SMEM)] * scalars
                + [pl.BlockSpec(memory_space=pltpu.HBM)] * (len(operands) - scalars),
                out_specs=pl.BlockSpec(memory_space=pltpu.HBM),
                out_shape=jax.ShapeDtypeStruct(out_shape, jnp.float32),
                scratch_shapes=scratch,
                input_output_aliases=aliases,
                compiler_params=pltpu.CompilerParams(vmem_limit_bytes=vmem_limit),
                cost_estimate=cost(count, 2 * length, planes * length),
                name=name,
            )(*operands)

        def room(*shape):
            return pltpu.VMEM(shape, jnp.float32)

        def sems(count):
            return pltpu.SemaphoreType.DMA((count,))

        def exchange(values):
            return lax.all_to_all(values, "plane", split_axis=0, concat_axis=0, tiled=True)

        def forward(bounds, batch, *filled):
            count = len(batch)
            return call(
                lambda *refs: forward_kernel(length, planes, count, *refs),
                "forward",
                count,
                (bounds, targets, *forward_matrices, *batch, *filled),
                (shards, bands, group, length),
                [room(*fields), right, left, room(count, *slab), room(count, *packed)]
                + [sems(3), sems(count), sems(count)],
                scalars=1,
                aliases={4 + count: 0} if filled else {},
            )

        def middle(values):
            count = values.shape[1]
            return call(
                lambda *refs: middle_kernel(length, planes, count, *refs),
                "middle",
                count,
                (values, grid_kernel, *middle_matrices),
                (shards, count, group, length),
                [room(count, *packed), room(planes, length, length), left, left]
                + [room(count, *packed)]
                + [sems(3), sems(count), sems(count)],
            )

        def backward(values, batch):
            count = len(batch)
            return call(
                lambda *refs: backward_kernel(length, planes, -exact_share, count, *refs),
                "backward",
                count,
                (values, *backward_matrices, *batch),
                fields,
                [room(count, *packed), left, right, room(count, *slab), room(*fields)]
                + [sems(2), sems(count), sems(count)],
            )

        def move(values, pairs):
            return lax.ppermute(values, "band", pairs)

        below, above = move(sources, up), move(sources, down)
        far = move(sources, opposite)
        every = [sources, move(sources, swap)]
        core = lax.axis_index("band") % 2
        bounds = jnp.array([[0, 2], [2, 6], [6, 8]], jnp.int32)
        filled = forward(bounds[0], every)
        below, above, filled = lax.optimization_barrier((below, above, filled))
        every += [below, above, move(below, swap), move(above, swap)]
        filled = forward(bounds[1], every, filled)
        far, filled = lax.optimization_barrier((far, filled))
        every += [far, move(far, swap)]
        filled = forward(bounds[2], every, filled)
        filled, grid_kernel = lax.optimization_barrier((filled, grid_kernel))
        here = exchange(middle(exchange(filled)))
        return backward(here, every)

    return jax.shard_map(
        on_device,
        mesh=mesh,
        in_specs=(
            P("band", "plane", None, None),
            P("band", "plane", None, None),
            P(None, "plane", None),
        ),
        out_specs=P("band", "plane", None, None),
        check_vma=False,
    )
```

time: 720 us -> 178 us (0.25)
  waiting for transfers between devices: 311 us -> 22.1 us
  matrix products: 171 us -> 0 us
  starting transfers between devices: 162 us -> 7.22 us
  blocking collectives: 0 us -> 114 us
  local copies, waits for them, and re-layouts: 55.7 us -> 0 us
  Pallas kernels: 0 us -> 31.6 us
  between operations: 13.4 us -> 0.04 us
    all_to_all x32 -> x0, waiting for transfers between devices: 270 us -> none  [the longest x8 77 us: potentials(): lax.all_to_all(imag_part, 'plane', split_axis=2, concat_axis=1, tiled=True)]
    dot_general x160 -> x0, matrix products: 171 us -> none  [transform_axis(): return jnp.einsum(pattern, values, matrix, precision=finest)]
    all_to_all x32 -> x0, starting transfers between devices: 162 us -> none  [the longest x8 42.3 us: potentials(): lax.all_to_all(real_part, 'plane', split_axis=2, concat_axis=1, tiled=True)]
    all_to_all x0 -> x2, blocking collectives: none -> 114 us  [exchange(): lax.all_to_all(values, 'plane', split_axis=0, concat_axis=0, tiled=True)]
    all_gather x1 -> x0, waiting for transfers between devices: 40.3 us -> none  [on_device(): everyone = lax.all_gather(sources, 'band', axis=0, tiled=True)]
    pallas_call x0 -> x5, Pallas kernels: none -> 31.6 us  [call(): pl.pallas_call(lambda *refs: body(*refs), in_specs=[pl.BlockSpec(memory_s...]
    ppermute x0 -> x7, waiting for transfers between devices: none -> 22.1 us  [move(): return lax.ppermute(values, 'band', pairs)]
    add x16 -> x0, local copies, waits for them, and re-layouts: 16.1 us -> none  [the longest x8 8.11 us: inverse(): transform_axis(imag_part, pattern, cosine_table)]
  transfers between devices with their start and end apart: 33 -> 7, of which waited for: 33 -> 6; matrix products, arithmetic and copies ran while one was open for 7% -> 1% of each run, Pallas kernels for 0% -> 6%
where the time goes in v2:
time: 178 us
  blocking collectives  114 us (64%)
  Pallas kernels  31.6 us (18%)
  waiting for transfers between devices  22.1 us (12%)
  starting transfers between devices  7.22 us (4%)
  other arithmetic  2.19 us (1%)
    all_to_all x2, blocking collectives, exchange(): lax.all_to_all(values, 'plane', split_axis=0, concat_axis=0, tiled=True)  114 us
    pallas_call x5, Pallas kernels, call(): pl.pallas_call(lambda *refs: body(*refs), in_specs=[pl.BlockSpec(memory_s...  31.6 us
    ppermute x7, waiting for transfers between devices, move(): return lax.ppermute(values, 'band', pairs)  22.1 us
    ppermute x7, starting transfers between devices, move(): return lax.ppermute(values, 'band', pairs)  7.22 us
  transfers between devices with their start and end apart: 7, of which 6 were waited for; matrix products, arithmetic and copies ran while one was open for 1% of the time, Pallas kernels for 6%

profile of v2, /device:TPU:8, one launch (start us, length us, event | category | flops | bytes accessed | tf_op | source)
XLA Modules:
  0.0 177.5 jit_solution(11358814301244961019)
XLA Ops:
  0.0 0.0 collective-permute-start
  0.0 6.3 %collective-permute-start.2 = (f32[1,4,128,128]{3,2,1,0:T(8,128)}, f32[1,4,128,128]{3,2,1,0:T(8,128)}, u32[]{:S(2)}, u32[]{:S(2)}) collective-permute-start(f32[1,4,128,128]{3,2,1,0:T(8,128)} %refs_3_.5), channel_id=1, source_target_pairs={{0,192},{32,224},{64,0},{96,32},{128,64},{160,96},{192,128},{224,1... | collective-permute-start | bytes 786440 | tf_op jit(solution)/shard_map/ppermute | solution.py:358
  6.3 0.0 collective-permute-start.1
  6.3 0.5 iota_multiply_fusion.refs_0_
  6.8 0.0 collective-permute-done.refs_5_.refs_4_
  6.8 4.7 %forward.3.refs_10_ = f32[32,8,32,128]{3,2,1,0:T(8,128)} custom-call(s32[2]{0:T(128)} %iota_multiply_fusion.refs_0_, f32[2,4,128,128]{3,2,1,0:T(8,128)} %refs_1_.6, bf16[768,256]{1,0:T(8,128)(2,1)} %constant.16.clone.refs_2_, bf16[256,768]{1,0:T(8,128)(2,1)} %constant.17.clone.refs_3_, f32[1,4,128,128]{3,2,1,0:T(8,128)} %refs_3_.5, ...), custom_call_target="tpu_custom_call" | custom-call | flops 805306368 | bytes 3145728 | tf_op jit(solution)/shard_map/forward/pallas_call | solution.py:296
  11.5 7.0 %collective-permute-done.2.refs_7_.refs_6_ = f32[1,4,128,128]{3,2,1,0:T(8,128)} collective-permute-done((f32[1,4,128,128]{3,2,1,0:T(8,128)}, f32[1,4,128,128]{3,2,1,0:T(8,128)}, u32[]{:S(2)}, u32[]{:S(2)}) %collective-permute-start.2) | collective-permute-done | bytes 262176 | tf_op jit(solution)/shard_map/ppermute | solution.py:358
  18.5 3.8 %collective-permute-done.1.refs_6_.refs_5_ = f32[1,4,128,128]{3,2,1,0:T(8,128)} collective-permute-done((f32[1,4,128,128]{3,2,1,0:T(8,128)}, f32[1,4,128,128]{3,2,1,0:T(8,128)}, u32[]{:S(2)}, u32[]{:S(2)}) %collective-permute-start.1) | collective-permute-done | bytes 262176 | tf_op jit(solution)/shard_map/ppermute | solution.py:358
  22.3 0.0 collective-permute-start.3
  22.3 0.5 collective-permute-start.4
  22.9 0.4 collective-permute-start.5
  23.3 1.0 collective-permute-done.3.refs_8_.refs_7_
  24.2 0.4 collective-permute-done.4.refs_9_.refs_8_
  24.6 6.5 %forward.4.refs_12_ = f32[32,8,32,128]{3,2,1,0:T(8,128)} custom-call(s32[2]{0:T(128)} %constant.31.refs_0_, f32[2,4,128,128]{3,2,1,0:T(8,128)} %refs_1_.6, bf16[768,256]{1,0:T(8,128)(2,1)} %constant.16.clone.refs_2_, bf16[256,768]{1,0:T(8,128)(2,1)} %constant.17.clone.refs_3_, f32[1,4,128,128]{3,2,1,0:T(8,128)} %refs_3_.5, ...), custom_call_target="tpu_custom_call", output_to_operand_aliasing={{}: (10, {})} | custom-call | flops 2415919104 | bytes 9437184 | tf_op jit(solution)/shard_map/forward/pallas_call | solution.py:296
  31.2 9.8 %collective-permute-done.5.refs_10_.refs_9_ = f32[1,4,128,128]{3,2,1,0:T(8,128)} collective-permute-done((f32[1,4,128,128]{3,2,1,0:T(8,128)}, f32[1,4,128,128]{3,2,1,0:T(8,128)}, u32[]{:S(2)}, u32[]{:S(2)}) %collective-permute-start.5) | collective-permute-done | bytes 262176 | tf_op jit(solution)/shard_map/ppermute | solution.py:358
  40.9 0.0 collective-permute-start.6
  40.9 1.7 fusion.refs_1_
  42.6 0.2 collective-permute-done.6.refs_11_.refs_10_
  42.8 4.8 %forward.5 = f32[32,8,32,128]{3,2,1,0:T(8,128)} custom-call(s32[2]{0:T(128)} %constant.27.refs_0_, f32[2,4,128,128]{3,2,1,0:T(8,128)} %refs_1_.6, bf16[768,256]{1,0:T(8,128)(2,1)} %constant.16.clone.refs_2_, bf16[256,768]{1,0:T(8,128)(2,1)} %constant.17.clone.refs_3_, f32[1,4,128,128]{3,2,1,0:T(8,128)} %refs_3_.5, ...), custom_call_target="tpu_custom_call", output_to_operand_aliasing={{}: (12, {})} | custom-call | flops 3221225472 | bytes 12582912 | tf_op jit(solution)/shard_map/forward/pallas_call | solution.py:296
  47.6 58.5 %all_to_all.10.refs_0_ = f32[32,8,32,128]{3,2,1,0:T(8,128)} all-to-all(f32[32,8,32,128]{3,2,1,0:T(8,128)} %forward.5), channel_id=1, replica_groups=mesh['band'=8,'plane'=32] {'plane'}, dimensions={0} | all-to-all | bytes 8388608 | tf_op jit(solution)/shard_map/all_to_all | solution.py:316
  106.1 7.4 %middle.1 = f32[32,8,32,128]{3,2,1,0:T(8,128)} custom-call(f32[32,8,32,128]{3,2,1,0:T(8,128)} %all_to_all.10.refs_0_, f32[4,128,128]{2,1,0:T(8,128)} %fusion.refs_1_, bf16[256,768]{1,0:T(8,128)(2,1)} %constant.18.clone.refs_2_, bf16[256,768]{1,0:T(8,128)(2,1)} %constant.19.clone.refs_3_), custom_call_target="tpu_custom_call" | custom-call | flops 3221225472 | bytes 12582912 | tf_op jit(solution)/shard_map/middle/pallas_call | solution.py:296
  113.6 55.8 %all_to_all.11.refs_0_ = f32[32,8,32,128]{3,2,1,0:T(8,128)} all-to-all(f32[32,8,32,128]{3,2,1,0:T(8,128)} %middle.1), channel_id=1, replica_groups=mesh['band'=8,'plane'=32] {'plane'}, dimensions={0} | all-to-all | bytes 8388608 | tf_op jit(solution)/shard_map/all_to_all | solution.py:316
  169.4 8.2 %backward.1 = f32[2,4,128,128]{3,2,1,0:T(8,128)} custom-call(f32[32,8,32,128]{3,2,1,0:T(8,128)} %all_to_all.11.refs_0_, bf16[256,768]{1,0:T(8,128)(2,1)} %constant.20.clone.refs_1_, bf16[768,256]{1,0:T(8,128)(2,1)} %constant.21.clone.refs_2_, f32[1,4,128,128]{3,2,1,0:T(8,128)} %refs_3_.5, f32[1,4,128,128]{3,2,1,0:T(8,128)} %collective-permute-done.refs_5_.refs_4_, ...), custom_call_target="tpu_custom_call" | custom-call | flops 3221225472 | bytes 12582912 | tf_op jit(solution)/shard_map/backward/pallas_call | solution.py:296
Async XLA Ops:
  0.0 6.8 %collective-permute-start = (f32[1,4,128,128]{3,2,1,0:T(8,128)}, f32[1,4,128,128]{3,2,1,0:T(8,128)}, u32[]{:S(2)}, u32[]{:S(2)}) collective-permute-start(f32[1,4,128,128]{3,2,1,0:T(8,128)} %refs_3_.5), channel_id=1, source_target_pairs={{0,32},{32,0},{64,96},{96,64},{128,160},{160,128},{192,224},{224,1... | collective-permute-start | bytes 786440 | tf_op jit(solution)/shard_map/ppermute | solution.py:358
  0.0 18.5 %collective-permute-start.2 = (f32[1,4,128,128]{3,2,1,0:T(8,128)}, f32[1,4,128,128]{3,2,1,0:T(8,128)}, u32[]{:S(2)}, u32[]{:S(2)}) collective-permute-start(f32[1,4,128,128]{3,2,1,0:T(8,128)} %refs_3_.5), channel_id=1, source_target_pairs={{0,192},{32,224},{64,0},{96,32},{128,64},{160,96},{192,128},{224,1... | collective-permute-start | bytes 786440 | tf_op jit(solution)/shard_map/ppermute | solution.py:358
  6.3 16.0 %collective-permute-start.1 = (f32[1,4,128,128]{3,2,1,0:T(8,128)}, f32[1,4,128,128]{3,2,1,0:T(8,128)}, u32[]{:S(2)}, u32[]{:S(2)}) collective-permute-start(f32[1,4,128,128]{3,2,1,0:T(8,128)} %refs_3_.5), channel_id=1, source_target_pairs={{0,64},{32,96},{64,128},{96,160},{128,192},{160,224},{192,0},{224,... | collective-permute-start | bytes 786440 | tf_op jit(solution)/shard_map/ppermute | solution.py:358
  22.3 1.9 %collective-permute-start.3 = (f32[1,4,128,128]{3,2,1,0:T(8,128)}, f32[1,4,128,128]{3,2,1,0:T(8,128)}, u32[]{:S(2)}, u32[]{:S(2)}) collective-permute-start(f32[1,4,128,128]{3,2,1,0:T(8,128)} %collective-permute-done.1.refs_6_.refs_5_), channel_id=1, source_target_pairs={{0,32},{32,0},{64,96},{96,64},{128,160},{160,128},{192,224},{224,1... | collective-permute-start | bytes 786440 | tf_op jit(solution)/shard_map/ppermute | solution.py:358
  22.3 2.2 %collective-permute-start.4 = (f32[1,4,128,128]{3,2,1,0:T(8,128)}, f32[1,4,128,128]{3,2,1,0:T(8,128)}, u32[]{:S(2)}, u32[]{:S(2)}) collective-permute-start(f32[1,4,128,128]{3,2,1,0:T(8,128)} %collective-permute-done.2.refs_7_.refs_6_), channel_id=1, source_target_pairs={{0,32},{32,0},{64,96},{96,64},{128,160},{160,128},{192,224},{224,1... | collective-permute-start | bytes 786440 | tf_op jit(solution)/shard_map/ppermute | solution.py:358
  22.9 18.1 %collective-permute-start.5 = (f32[1,4,128,128]{3,2,1,0:T(8,128)}, f32[1,4,128,128]{3,2,1,0:T(8,128)}, u32[]{:S(2)}, u32[]{:S(2)}) collective-permute-start(f32[1,4,128,128]{3,2,1,0:T(8,128)} %refs_3_.5), channel_id=1, source_target_pairs={{0,128},{32,160},{64,192},{96,224},{128,0},{160,32},{192,64},{224,... | collective-permute-start | bytes 786440 | tf_op jit(solution)/shard_map/ppermute | solution.py:358
  40.9 1.9 %collective-permute-start.6 = (f32[1,4,128,128]{3,2,1,0:T(8,128)}, f32[1,4,128,128]{3,2,1,0:T(8,128)}, u32[]{:S(2)}, u32[]{:S(2)}) collective-permute-start(f32[1,4,128,128]{3,2,1,0:T(8,128)} %collective-permute-done.5.refs_10_.refs_9_), channel_id=1, source_target_pairs={{0,32},{32,0},{64,96},{96,64},{128,160},{160,128},{192,224},{224,1... | collective-permute-start | bytes 786440 | tf_op jit(solution)/shard_map/ppermute | solution.py:358

commit v3 on v2

--- a/solution.py
+++ b/solution.py
@@ -21,12 +21,12 @@
 
 def left_form(matrix):
     high, low = halves(matrix)
-    return np.concatenate([high, high, low], axis=1)
+    return np.concatenate([high, low], axis=1)
 
 
 def right_form(matrix):
     high, low = halves(matrix)
-    return np.concatenate([high, high, low], axis=0)
+    return np.concatenate([high, low], axis=0)
 
 
 def dft_matrices(length, planes):
@@ -51,14 +51,18 @@
 
 def from_left(matrix_ref, values):
     high, low = split(values)
+    inner = values.shape[0]
+    matrix = jnp.concatenate([matrix_ref[:, :inner], matrix_ref[...]], axis=1)
     stack = jnp.concatenate([high, low, high], axis=0)
-    return jnp.dot(matrix_ref[...], stack, preferred_element_type=jnp.float32)
+    return jnp.dot(matrix, stack, preferred_element_type=jnp.float32)
 
 
 def from_right(values, matrix_ref):
     high, low = split(values)
+    inner = values.shape[1]
+    matrix = jnp.concatenate([matrix_ref[:inner], matrix_ref[...]], axis=0)
     stack = jnp.concatenate([high, low, high], axis=1)
-    return jnp.dot(stack, matrix_ref[...], preferred_element_type=jnp.float32)
+    return jnp.dot(stack, matrix, preferred_element_type=jnp.float32)
 
 
 def fetch(pairs, sems):
@@ -274,9 +278,8 @@
     shards = mesh.shape["plane"]
     bands = mesh.shape["band"]
     swap = [(b, b ^ 1) for b in range(bands)]
-    up = [(b, (b + 2) % bands) for b in range(bands)]
-    down = [(b, (b - 2) % bands) for b in range(bands)]
-    opposite = [(b, (b + 4) % bands) for b in range(bands)]
+    one_way = [(b, (b + (-2 if b % 2 else 2)) % bands) for b in range(bands)]
+    other_way = [(to, b) for b, to in one_way]
 
     def on_device(targets, sources, kernel):
         length = targets.shape[-1]
@@ -288,8 +291,8 @@
         slab = (planes, length, length)
         fields = (2,) + slab
         packed = (shards, group, length)
-        left = pltpu.VMEM((2 * length, 6 * length), jnp.bfloat16)
-        right = pltpu.VMEM((6 * length, 2 * length), jnp.bfloat16)
+        left = pltpu.VMEM((2 * length, 4 * length), jnp.bfloat16)
+        right = pltpu.VMEM((4 * length, 2 * length), jnp.bfloat16)
         grid_kernel = (kernel * (1.0 / float(length) ** 3)).transpose(1, 0, 2)
 
         def call(body, name, count, operands, out_shape, scratch, scalars=0, aliases={}):
@@ -320,7 +323,7 @@
             return call(
                 lambda *refs: forward_kernel(length, planes, count, *refs),
                 "forward",
-                count,
+                0,
                 (bounds, targets, *forward_matrices, *batch, *filled),
                 (shards, bands, group, length),
                 [room(*fields), right, left, room(count, *slab), room(count, *packed)]
@@ -357,19 +360,19 @@
         def move(values, pairs):
             return lax.ppermute(values, "band", pairs)
 
-        below, above = move(sources, up), move(sources, down)
-        far = move(sources, opposite)
+        near, other = move(sources, one_way), move(sources, other_way)
         every = [sources, move(sources, swap)]
-        core = lax.axis_index("band") % 2
         bounds = jnp.array([[0, 2], [2, 6], [6, 8]], jnp.int32)
         filled = forward(bounds[0], every)
-        below, above, filled = lax.optimization_barrier((below, above, filled))
-        every += [below, above, move(below, swap), move(above, swap)]
+        near, filled, grid_kernel = lax.optimization_barrier((near, filled, grid_kernel))
+        far = move(near, one_way)
+        near_too = move(near, swap)
+        other, near_too = lax.optimization_barrier((other, near_too))
+        every += [near, near_too, other, move(other, swap)]
         filled = forward(bounds[1], every, filled)
         far, filled = lax.optimization_barrier((far, filled))
         every += [far, move(far, swap)]
         filled = forward(bounds[2], every, filled)
-        filled, grid_kernel = lax.optimization_barrier((filled, grid_kernel))
         here = exchange(middle(exchange(filled)))
         return backward(here, every)
 

time: 178 us -> 168 us (0.944)
  waiting for transfers between devices: 22.1 us -> 12.6 us
    ppermute x7, waiting for transfers between devices: 22.1 us -> 12.6 us  [move(): return lax.ppermute(values, 'band', pairs)]
  transfers between devices with their start and end apart: 7 -> 7, of which waited for: 6 -> 5; matrix products, arithmetic and copies ran while one was open for 1% -> 1% of each run, Pallas kernels for 6% -> 7%
where the time goes in v3:
time: 168 us
  blocking collectives  114 us (68%)
  Pallas kernels  31.2 us (19%)
  waiting for transfers between devices  12.6 us (8%)
  starting transfers between devices  7.55 us (4%)
  other arithmetic  2.19 us (1%)
    all_to_all x2, blocking collectives, exchange(): lax.all_to_all(values, 'plane', split_axis=0, concat_axis=0, tiled=True)  114 us
    pallas_call x5, Pallas kernels, call(): pl.pallas_call(lambda *refs: body(*refs), in_specs=[pl.BlockSpec(memory_s...  31.2 us
    ppermute x7, waiting for transfers between devices, move(): return lax.ppermute(values, 'band', pairs)  12.6 us
    ppermute x7, starting transfers between devices, move(): return lax.ppermute(values, 'band', pairs)  7.55 us
  transfers between devices with their start and end apart: 7, of which 5 were waited for; matrix products, arithmetic and copies ran while one was open for 1% of the time, Pallas kernels for 7%

profile of v3, /device:TPU:8, one launch (start us, length us, event | category | flops | bytes accessed | tf_op | source)
XLA Modules:
  0.0 167.6 jit_solution(2916371997108050042)
XLA Ops:
  0.0 6.3 %collective-permute-start.2 = (f32[1,4,128,128]{3,2,1,0:T(8,128)}, f32[1,4,128,128]{3,2,1,0:T(8,128)}, u32[]{:S(2)}, u32[]{:S(2)}) collective-permute-start(f32[1,4,128,128]{3,2,1,0:T(8,128)} %refs_3_.5), channel_id=1, source_target_pairs={{64,0},{224,32},{128,64},{32,96},{192,128},{96,160},{0,192},{160,2... | collective-permute-start | bytes 786440 | tf_op jit(solution)/shard_map/ppermute | solution.py:361
  6.3 0.0 collective-permute-start.1
  6.3 0.0 collective-permute-start
  6.3 0.5 iota_multiply_fusion.refs_0_
  6.8 1.7 fusion.refs_1_
  8.5 0.0 collective-permute-done.refs_5_.refs_4_
  8.5 4.6 %forward.3.refs_10_ = f32[32,8,32,128]{3,2,1,0:T(8,128)} custom-call(s32[2]{0:T(128)} %iota_multiply_fusion.refs_0_, f32[2,4,128,128]{3,2,1,0:T(8,128)} %refs_1_.6, bf16[512,256]{1,0:T(8,128)(2,1)} %constant.16.clone.refs_2_, bf16[256,512]{1,0:T(8,128)(2,1)} %constant.17.clone.refs_3_, f32[1,4,128,128]{3,2,1,0:T(8,128)} %refs_3_.5, ...), custom_call_target="tpu_custom_call" | custom-call | tf_op jit(solution)/shard_map/forward/pallas_call | solution.py:299
  13.1 6.3 %collective-permute-done.1.refs_6_.refs_5_ = f32[1,4,128,128]{3,2,1,0:T(8,128)} collective-permute-done((f32[1,4,128,128]{3,2,1,0:T(8,128)}, f32[1,4,128,128]{3,2,1,0:T(8,128)}, u32[]{:S(2)}, u32[]{:S(2)}) %collective-permute-start.1) | collective-permute-done | bytes 262176 | tf_op jit(solution)/shard_map/ppermute | solution.py:361
  19.4 0.0 collective-permute-start.3
  19.4 0.0 collective-permute-done.2.refs_8_.refs_7_
  19.4 1.9 %collective-permute-done.3.refs_7_.refs_6_ = f32[1,4,128,128]{3,2,1,0:T(8,128)} collective-permute-done((f32[1,4,128,128]{3,2,1,0:T(8,128)}, f32[1,4,128,128]{3,2,1,0:T(8,128)}, u32[]{:S(2)}, u32[]{:S(2)}) %collective-permute-start.3) | collective-permute-done | bytes 262176 | tf_op jit(solution)/shard_map/ppermute | solution.py:361
  21.3 0.1 collective-permute-start.4
  21.4 1.1 collective-permute-start.5
  22.5 0.6 collective-permute-done.4.refs_9_.refs_8_
  23.2 6.5 %forward.4.refs_12_ = f32[32,8,32,128]{3,2,1,0:T(8,128)} custom-call(s32[2]{0:T(128)} %constant.31.refs_0_, f32[2,4,128,128]{3,2,1,0:T(8,128)} %refs_1_.6, bf16[512,256]{1,0:T(8,128)(2,1)} %constant.16.clone.refs_2_, bf16[256,512]{1,0:T(8,128)(2,1)} %constant.17.clone.refs_3_, f32[1,4,128,128]{3,2,1,0:T(8,128)} %refs_3_.5, ...), custom_call_target="tpu_custom_call", output_to_operand_aliasing={{}: (10, {})} | custom-call | tf_op jit(solution)/shard_map/forward/pallas_call | solution.py:299
  29.7 2.0 %collective-permute-done.5.refs_10_.refs_9_ = f32[1,4,128,128]{3,2,1,0:T(8,128)} collective-permute-done((f32[1,4,128,128]{3,2,1,0:T(8,128)}, f32[1,4,128,128]{3,2,1,0:T(8,128)}, u32[]{:S(2)}, u32[]{:S(2)}) %collective-permute-start.5) | collective-permute-done | bytes 262176 | tf_op jit(solution)/shard_map/ppermute | solution.py:361
  31.6 0.0 collective-permute-start.6
  31.6 1.9 %collective-permute-done.6.refs_11_.refs_10_ = f32[1,4,128,128]{3,2,1,0:T(8,128)} collective-permute-done((f32[1,4,128,128]{3,2,1,0:T(8,128)}, f32[1,4,128,128]{3,2,1,0:T(8,128)}, u32[]{:S(2)}, u32[]{:S(2)}) %collective-permute-start.6) | collective-permute-done | bytes 262176 | tf_op jit(solution)/shard_map/ppermute | solution.py:361
  33.5 4.7 %forward.5 = f32[32,8,32,128]{3,2,1,0:T(8,128)} custom-call(s32[2]{0:T(128)} %constant.27.refs_0_, f32[2,4,128,128]{3,2,1,0:T(8,128)} %refs_1_.6, bf16[512,256]{1,0:T(8,128)(2,1)} %constant.16.clone.refs_2_, bf16[256,512]{1,0:T(8,128)(2,1)} %constant.17.clone.refs_3_, f32[1,4,128,128]{3,2,1,0:T(8,128)} %refs_3_.5, ...), custom_call_target="tpu_custom_call", output_to_operand_aliasing={{}: (12, {})} | custom-call | tf_op jit(solution)/shard_map/forward/pallas_call | solution.py:299
  38.2 58.3 %all_to_all.10.refs_0_ = f32[32,8,32,128]{3,2,1,0:T(8,128)} all-to-all(f32[32,8,32,128]{3,2,1,0:T(8,128)} %forward.5), channel_id=1, replica_groups=mesh['band'=8,'plane'=32] {'plane'}, dimensions={0} | all-to-all | bytes 8388608 | tf_op jit(solution)/shard_map/all_to_all | solution.py:319
  96.5 7.4 %middle.1 = f32[32,8,32,128]{3,2,1,0:T(8,128)} custom-call(f32[32,8,32,128]{3,2,1,0:T(8,128)} %all_to_all.10.refs_0_, f32[4,128,128]{2,1,0:T(8,128)} %fusion.refs_1_, bf16[256,512]{1,0:T(8,128)(2,1)} %constant.18.clone.refs_2_, bf16[256,512]{1,0:T(8,128)(2,1)} %constant.19.clone.refs_3_), custom_call_target="tpu_custom_call" | custom-call | flops 3221225472 | bytes 12582912 | tf_op jit(solution)/shard_map/middle/pallas_call | solution.py:299
  103.9 55.7 %all_to_all.11.refs_0_ = f32[32,8,32,128]{3,2,1,0:T(8,128)} all-to-all(f32[32,8,32,128]{3,2,1,0:T(8,128)} %middle.1), channel_id=1, replica_groups=mesh['band'=8,'plane'=32] {'plane'}, dimensions={0} | all-to-all | bytes 8388608 | tf_op jit(solution)/shard_map/all_to_all | solution.py:319
  159.6 8.1 %backward.1 = f32[2,4,128,128]{3,2,1,0:T(8,128)} custom-call(f32[32,8,32,128]{3,2,1,0:T(8,128)} %all_to_all.11.refs_0_, bf16[256,512]{1,0:T(8,128)(2,1)} %constant.20.clone.refs_1_, bf16[512,256]{1,0:T(8,128)(2,1)} %constant.21.clone.refs_2_, f32[1,4,128,128]{3,2,1,0:T(8,128)} %refs_3_.5, f32[1,4,128,128]{3,2,1,0:T(8,128)} %collective-permute-done.refs_5_.refs_4_, ...), custom_call_target="tpu_custom_call" | custom-call | flops 3221225472 | bytes 12582912 | tf_op jit(solution)/shard_map/backward/pallas_call | solution.py:299
Async XLA Ops:
  0.0 19.4 %collective-permute-start.2 = (f32[1,4,128,128]{3,2,1,0:T(8,128)}, f32[1,4,128,128]{3,2,1,0:T(8,128)}, u32[]{:S(2)}, u32[]{:S(2)}) collective-permute-start(f32[1,4,128,128]{3,2,1,0:T(8,128)} %refs_3_.5), channel_id=1, source_target_pairs={{64,0},{224,32},{128,64},{32,96},{192,128},{96,160},{0,192},{160,2... | collective-permute-start | bytes 786440 | tf_op jit(solution)/shard_map/ppermute | solution.py:361
  6.3 13.1 %collective-permute-start.1 = (f32[1,4,128,128]{3,2,1,0:T(8,128)}, f32[1,4,128,128]{3,2,1,0:T(8,128)}, u32[]{:S(2)}, u32[]{:S(2)}) collective-permute-start(f32[1,4,128,128]{3,2,1,0:T(8,128)} %refs_3_.5), channel_id=1, source_target_pairs={{0,64},{32,224},{64,128},{96,32},{128,192},{160,96},{192,0},{224,1... | collective-permute-start | bytes 786440 | tf_op jit(solution)/shard_map/ppermute | solution.py:361
  6.3 2.2 %collective-permute-start = (f32[1,4,128,128]{3,2,1,0:T(8,128)}, f32[1,4,128,128]{3,2,1,0:T(8,128)}, u32[]{:S(2)}, u32[]{:S(2)}) collective-permute-start(f32[1,4,128,128]{3,2,1,0:T(8,128)} %refs_3_.5), channel_id=1, source_target_pairs={{0,32},{32,0},{64,96},{96,64},{128,160},{160,128},{192,224},{224,1... | collective-permute-start | bytes 786440 | tf_op jit(solution)/shard_map/ppermute | solution.py:361
  19.4 1.9 %collective-permute-start.3 = (f32[1,4,128,128]{3,2,1,0:T(8,128)}, f32[1,4,128,128]{3,2,1,0:T(8,128)}, u32[]{:S(2)}, u32[]{:S(2)}) collective-permute-start(f32[1,4,128,128]{3,2,1,0:T(8,128)} %collective-permute-done.1.refs_6_.refs_5_), channel_id=1, source_target_pairs={{0,32},{32,0},{64,96},{96,64},{128,160},{160,128},{192,224},{224,1... | collective-permute-start | bytes 786440 | tf_op jit(solution)/shard_map/ppermute | solution.py:361
  21.3 1.9 %collective-permute-start.4 = (f32[1,4,128,128]{3,2,1,0:T(8,128)}, f32[1,4,128,128]{3,2,1,0:T(8,128)}, u32[]{:S(2)}, u32[]{:S(2)}) collective-permute-start(f32[1,4,128,128]{3,2,1,0:T(8,128)} %collective-permute-done.2.refs_8_.refs_7_), channel_id=1, source_target_pairs={{0,32},{32,0},{64,96},{96,64},{128,160},{160,128},{192,224},{224,1... | collective-permute-start | bytes 786440 | tf_op jit(solution)/shard_map/ppermute | solution.py:361
  21.4 10.2 %collective-permute-start.5 = (f32[1,4,128,128]{3,2,1,0:T(8,128)}, f32[1,4,128,128]{3,2,1,0:T(8,128)}, u32[]{:S(2)}, u32[]{:S(2)}) collective-permute-start(f32[1,4,128,128]{3,2,1,0:T(8,128)} %collective-permute-done.1.refs_6_.refs_5_), channel_id=1, source_target_pairs={{0,64},{32,224},{64,128},{96,32},{128,192},{160,96},{192,0},{224,1... | collective-permute-start | bytes 786440 | tf_op jit(solution)/shard_map/ppermute | solution.py:361
  31.6 1.9 %collective-permute-start.6 = (f32[1,4,128,128]{3,2,1,0:T(8,128)}, f32[1,4,128,128]{3,2,1,0:T(8,128)}, u32[]{:S(2)}, u32[]{:S(2)}) collective-permute-start(f32[1,4,128,128]{3,2,1,0:T(8,128)} %collective-permute-done.5.refs_10_.refs_9_), channel_id=1, source_target_pairs={{0,32},{32,0},{64,96},{96,64},{128,160},{160,128},{192,224},{224,1... | collective-permute-start | bytes 786440 | tf_op jit(solution)/shard_map/ppermute | solution.py:361

commit v4 on v3

--- a/solution.py
+++ b/solution.py
@@ -10,7 +10,7 @@
 from jax.sharding import PartitionSpec as P
 
 exact_share = 0.25
-vmem_limit = 64 * 1024 * 1024
+vmem_limit = 28 * 1024 * 1024
 
 
 def halves(matrix):

time: 168 us -> 159 us (0.946)
  Pallas kernels: 31.2 us -> 21.1 us
  local copies, waits for them, and re-layouts: 0 us -> 3.94 us
  blocking collectives: 114 us -> 112 us
    pallas_call x5, Pallas kernels: 31.2 us -> 21.1 us  [call(): pl.pallas_call(lambda *refs: body(*refs), in_specs=[pl.BlockSpec(memory_s...]
    unnamed x0 -> x24, local copies, waits for them, and re-layouts: none -> 3.94 us
    all_to_all x2, blocking collectives: 114 us -> 112 us  [exchange(): lax.all_to_all(values, 'plane', split_axis=0, concat_axis=0, tiled=True)]
  transfers between devices with their start and end apart: 7 -> 7, of which waited for: 5 -> 6; matrix products, arithmetic and copies ran while one was open for 1% -> 1% of each run, Pallas kernels for 7% -> 5%
where the time goes in v4:
time: 159 us; the launch traced here: 158 us
  blocking collectives  112 us (70%)
  Pallas kernels  21.1 us (13%)
  waiting for transfers between devices  12.5 us (8%)
  starting transfers between devices  7.55 us (5%)
  local copies, waits for them, and re-layouts  3.94 us (2%)
    all_to_all x2, blocking collectives, exchange(): lax.all_to_all(values, 'plane', split_axis=0, concat_axis=0, tiled=True)  112 us
    pallas_call x5, Pallas kernels, call(): pl.pallas_call(lambda *refs: body(*refs), in_specs=[pl.BlockSpec(memory_s...  21.1 us
    ppermute x7, waiting for transfers between devices, move(): return lax.ppermute(values, 'band', pairs)  12.5 us
    ppermute x7, starting transfers between devices, move(): return lax.ppermute(values, 'band', pairs)  7.55 us
    unnamed x24, local copies, waits for them, and re-layouts  3.94 us
  transfers between devices with their start and end apart: 7, of which 6 were waited for; matrix products, arithmetic and copies ran while one was open for 1% of the time, Pallas kernels for 5%

profile of v4, /device:TPU:8, one launch (start us, length us, event | category | flops | bytes accessed | tf_op | source)
XLA Modules:
  0.0 158.3 jit_solution(17688319271337679770)
XLA Ops:
  0.0 0.0 copy-start.7
  0.0 0.0 copy-start.1
  0.0 6.3 %collective-permute-start.2 = (f32[1,4,128,128]{3,2,1,0:T(8,128)}, f32[1,4,128,128]{3,2,1,0:T(8,128)S(1)}, u32[]{:S(2)}, u32[]{:S(2)}) collective-permute-start(f32[1,4,128,128]{3,2,1,0:T(8,128)} %refs_3_.5), channel_id=1, source_target_pairs={{64,0},{224,32},{128,64},{32,96},{192,128},{96,160},{0,192},{160,2... | collective-permute-start | bytes 786440 | tf_op jit(solution)/shard_map/ppermute | solution.py:361
  6.3 0.0 collective-permute-start.1
  6.3 0.0 collective-permute-start
  6.3 1.0 fusion.refs_1_
  7.3 0.8 collective-permute-done.refs_5_.refs_4_
  8.1 0.0 copy-start
  8.1 1.0 copy-done
  9.1 0.0 copy-start.2
  9.1 0.9 copy-done.2
  10.0 0.0 copy-start.4
  10.1 0.9 copy-done.4
  11.0 0.0 copy-start.5
  11.0 0.9 copy-done.5
  11.9 0.0 copy-start.3
  12.0 2.7 %forward.3.refs_10_ = f32[32,8,32,128]{3,2,1,0:T(8,128)S(1)} custom-call(s32[2]{0:T(128)S(1)} %iota_multiply_fusion.refs_0_, f32[2,4,128,128]{3,2,1,0:T(8,128)S(1)} %copy-done, bf16[512,256]{1,0:T(8,128)(2,1)S(1)} %copy-done.5, bf16[256,512]{1,0:T(8,128)(2,1)S(1)} %copy-done.4, f32[1,4,128,128]{3,2,1,0:T(8,128)S(1)} %copy-done.2, ...), custom_call_target="tpu_custom_call" | custom-call | tf_op jit(solution)/shard_map/forward/pallas_call | solution.py:299
  14.6 0.0 copy-start.6
  14.6 4.7 %collective-permute-done.1.refs_6_.refs_5_ = f32[1,4,128,128]{3,2,1,0:T(8,128)S(1)} collective-permute-done((f32[1,4,128,128]{3,2,1,0:T(8,128)}, f32[1,4,128,128]{3,2,1,0:T(8,128)S(1)}, u32[]{:S(2)}, u32[]{:S(2)}) %collective-permute-start.1) | collective-permute-done | bytes 262176 | tf_op jit(solution)/shard_map/ppermute | solution.py:361
  19.3 0.0 collective-permute-start.3
  19.3 0.0 collective-permute-done.2.refs_8_.refs_7_
  19.3 1.5 collective-permute-done.3.refs_7_.refs_6_
  20.9 0.1 collective-permute-start.4
  21.0 1.1 collective-permute-start.5
  22.1 0.3 collective-permute-done.4.refs_9_.refs_8_
  22.4 0.0 copy-done.7
  22.4 0.0 copy-done.1
  22.4 0.0 copy-done.3
  22.4 4.7 %forward.4.refs_12_ = f32[32,8,32,128]{3,2,1,0:T(8,128)S(1)} custom-call(s32[2]{0:T(128)S(1)} %copy-done.7, f32[2,4,128,128]{3,2,1,0:T(8,128)S(1)} %copy-done.1, bf16[512,256]{1,0:T(8,128)(2,1)S(1)} %copy-done.5, bf16[256,512]{1,0:T(8,128)(2,1)S(1)} %copy-done.4, f32[1,4,128,128]{3,2,1,0:T(8,128)S(1)} %copy-done.3, ...), custom_call_target="tpu_custom_call", output_to_operand_aliasing={{}: (10, {})} | custom-call | tf_op jit(solution)/shard_map/forward/pallas_call | solution.py:299
  27.1 3.7 %collective-permute-done.5.refs_10_.refs_9_ = f32[1,4,128,128]{3,2,1,0:T(8,128)S(1)} collective-permute-done((f32[1,4,128,128]{3,2,1,0:T(8,128)S(1)}, f32[1,4,128,128]{3,2,1,0:T(8,128)S(1)}, u32[]{:S(2)}, u32[]{:S(2)}) %collective-permute-start.5) | collective-permute-done | bytes 262176 | tf_op jit(solution)/shard_map/ppermute | solution.py:361
  30.8 0.0 collective-permute-start.6
  30.9 1.5 collective-permute-done.6.refs_11_.refs_10_
  32.4 0.0 copy-done.6
  32.4 2.8 %forward.5 = f32[32,8,32,128]{3,2,1,0:T(8,128)S(1)} custom-call(s32[2]{0:T(128)S(1)} %copy-done.6, f32[2,4,128,128]{3,2,1,0:T(8,128)S(1)} %copy-done.1, bf16[512,256]{1,0:T(8,128)(2,1)S(1)} %copy-done.5, bf16[256,512]{1,0:T(8,128)(2,1)S(1)} %copy-done.4, f32[1,4,128,128]{3,2,1,0:T(8,128)S(1)} %copy-done.3, ...), custom_call_target="tpu_custom_call", output_to_operand_aliasing={{}: (12, {})} | custom-call | tf_op jit(solution)/shard_map/forward/pallas_call | solution.py:299
  35.2 0.0 copy-start.10
  35.2 0.0 copy-start.11
  35.2 58.1 %all_to_all.10.refs_0_ = f32[32,8,32,128]{3,2,1,0:T(8,128)S(1)} all-to-all(f32[32,8,32,128]{3,2,1,0:T(8,128)S(1)} %forward.5), channel_id=1, replica_groups=mesh['band'=8,'plane'=32] {'plane'}, dimensions={0} | all-to-all | bytes 8388608 | tf_op jit(solution)/shard_map/all_to_all | solution.py:319
  93.3 0.0 copy-done.10
  93.3 0.0 copy-done.11
  93.3 4.9 %middle.1 = f32[32,8,32,128]{3,2,1,0:T(8,128)S(1)} custom-call(f32[32,8,32,128]{3,2,1,0:T(8,128)S(1)} %all_to_all.10.refs_0_, f32[4,128,128]{2,1,0:T(8,128)S(1)} %fusion.refs_1_, bf16[256,512]{1,0:T(8,128)(2,1)S(1)} %copy-done.11, bf16[256,512]{1,0:T(8,128)(2,1)S(1)} %copy-done.10), custom_call_target="tpu_custom_call" | custom-call | flops 3221225472 | bytes 12582912 | tf_op jit(solution)/shard_map/middle/pallas_call | solution.py:299
  98.3 0.0 copy-start.8
  98.3 0.0 copy-start.9
  98.3 54.0 %all_to_all.11.refs_0_ = f32[32,8,32,128]{3,2,1,0:T(8,128)S(1)} all-to-all(f32[32,8,32,128]{3,2,1,0:T(8,128)S(1)} %middle.1), channel_id=1, replica_groups=mesh['band'=8,'plane'=32] {'plane'}, dimensions={0} | all-to-all | bytes 8388608 | tf_op jit(solution)/shard_map/all_to_all | solution.py:319
  152.3 0.0 copy-done.8
  152.3 0.0 copy-done.9
  152.3 6.0 %backward.1 = f32[2,4,128,128]{3,2,1,0:T(8,128)} custom-call(f32[32,8,32,128]{3,2,1,0:T(8,128)S(1)} %all_to_all.11.refs_0_, bf16[256,512]{1,0:T(8,128)(2,1)S(1)} %copy-done.9, bf16[512,256]{1,0:T(8,128)(2,1)S(1)} %copy-done.8, f32[1,4,128,128]{3,2,1,0:T(8,128)S(1)} %copy-done.3, f32[1,4,128,128]{3,2,1,0:T(8,128)S(1)} %collective-permute-done.refs_5_.refs_4_, ...), custom_call_target="tpu_custom_call" | custom-call | flops 3221225472 | bytes 12582912 | tf_op jit(solution)/shard_map/backward/pallas_call | solution.py:299
  (1 shorter events, 0.0 us)
Async XLA Ops:
  0.0 22.4 %copy-start.7 = (s32[2]{0:T(128)S(1)}, s32[2]{0:T(128)}, u32[]{:S(2)}) copy-start(s32[2]{0:T(128)} %constant.31.refs_0_) | copy-start | bytes 28
  0.0 22.4 %copy-start.1 = (f32[2,4,128,128]{3,2,1,0:T(8,128)S(1)}, f32[2,4,128,128]{3,2,1,0:T(8,128)}, u32[]{:S(2)}) copy-start(f32[2,4,128,128]{3,2,1,0:T(8,128)} %refs_1_.6) | copy-start | bytes 1572868
  0.0 19.3 %collective-permute-start.2 = (f32[1,4,128,128]{3,2,1,0:T(8,128)}, f32[1,4,128,128]{3,2,1,0:T(8,128)S(1)}, u32[]{:S(2)}, u32[]{:S(2)}) collective-permute-start(f32[1,4,128,128]{3,2,1,0:T(8,128)} %refs_3_.5), channel_id=1, source_target_pairs={{64,0},{224,32},{128,64},{32,96},{192,128},{96,160},{0,192},{160,2... | collective-permute-start | bytes 786440 | tf_op jit(solution)/shard_map/ppermute | solution.py:361
  6.3 13.0 %collective-permute-start.1 = (f32[1,4,128,128]{3,2,1,0:T(8,128)}, f32[1,4,128,128]{3,2,1,0:T(8,128)S(1)}, u32[]{:S(2)}, u32[]{:S(2)}) collective-permute-start(f32[1,4,128,128]{3,2,1,0:T(8,128)} %refs_3_.5), channel_id=1, source_target_pairs={{0,64},{32,224},{64,128},{96,32},{128,192},{160,96},{192,0},{224,1... | collective-permute-start | bytes 786440 | tf_op jit(solution)/shard_map/ppermute | solution.py:361
  6.3 1.7 %collective-permute-start = (f32[1,4,128,128]{3,2,1,0:T(8,128)}, f32[1,4,128,128]{3,2,1,0:T(8,128)S(1)}, u32[]{:S(2)}, u32[]{:S(2)}) collective-permute-start(f32[1,4,128,128]{3,2,1,0:T(8,128)} %refs_3_.5), channel_id=1, source_target_pairs={{0,32},{32,0},{64,96},{96,64},{128,160},{160,128},{192,224},{224,1... | collective-permute-start | bytes 786440 | tf_op jit(solution)/shard_map/ppermute | solution.py:361
  8.1 1.0 copy-start
  9.1 0.9 copy-start.2
  10.0 0.9 copy-start.4
  11.0 0.9 copy-start.5
  11.9 10.5 %copy-start.3 = (f32[1,4,128,128]{3,2,1,0:T(8,128)S(1)}, f32[1,4,128,128]{3,2,1,0:T(8,128)}, u32[]{:S(2)}) copy-start(f32[1,4,128,128]{3,2,1,0:T(8,128)} %refs_3_.5) | copy-start | bytes 786436
  14.6 17.8 %copy-start.6 = (s32[2]{0:T(128)S(1)}, s32[2]{0:T(128)}, u32[]{:S(2)}) copy-start(s32[2]{0:T(128)} %constant.27.refs_0_) | copy-start | bytes 28
  19.3 1.5 collective-permute-start.3
  20.9 1.5 collective-permute-start.4
  21.0 9.8 %collective-permute-start.5 = (f32[1,4,128,128]{3,2,1,0:T(8,128)S(1)}, f32[1,4,128,128]{3,2,1,0:T(8,128)S(1)}, u32[]{:S(2)}, u32[]{:S(2)}) collective-permute-start(f32[1,4,128,128]{3,2,1,0:T(8,128)S(1)} %collective-permute-done.1.refs_6_.refs_5_), channel_id=1, source_target_pairs={{0,64},{32,224},{64,128},{96,32},{128,192},{160,96},{192,0},{224,1... | collective-permute-start | bytes 786440 | tf_op jit(solution)/shard_map/ppermute | solution.py:361
  30.8 1.5 collective-permute-start.6
  35.2 58.1 %copy-start.10 = (bf16[256,512]{1,0:T(8,128)(2,1)S(1)}, bf16[256,512]{1,0:T(8,128)(2,1)}, u32[]{:S(2)}) copy-start(bf16[256,512]{1,0:T(8,128)(2,1)} %constant.19.clone.refs_3_) | copy-start | bytes 786436
  35.2 58.1 %copy-start.11 = (bf16[256,512]{1,0:T(8,128)(2,1)S(1)}, bf16[256,512]{1,0:T(8,128)(2,1)}, u32[]{:S(2)}) copy-start(bf16[256,512]{1,0:T(8,128)(2,1)} %constant.18.clone.refs_2_) | copy-start | bytes 786436
  98.3 54.0 %copy-start.8 = (bf16[512,256]{1,0:T(8,128)(2,1)S(1)}, bf16[512,256]{1,0:T(8,128)(2,1)}, u32[]{:S(2)}) copy-start(bf16[512,256]{1,0:T(8,128)(2,1)} %constant.21.clone.refs_2_) | copy-start | bytes 786436
  98.3 54.0 %copy-start.9 = (bf16[256,512]{1,0:T(8,128)(2,1)S(1)}, bf16[256,512]{1,0:T(8,128)(2,1)}, u32[]{:S(2)}) copy-start(bf16[256,512]{1,0:T(8,128)(2,1)} %constant.20.clone.refs_1_) | copy-start | bytes 786436
